TPU v7x, 32 devices: a whole 2x2x4 slice. The times are simulated.
32 devices in a mesh: loop: 8 (over y, x, core), tp: 4 (over z).
Axes of the slice: x: 2, y: 2, z: 4, core: 2. Of those that a mesh axis runs over, the one named last changes fastest.
Arguments:
- queries: bfloat16 [2048, 4096], P('loop', 'tp'), may hold values from -8 to 8
- key_values: bfloat16 [2048, 1024], P('loop', 'tp'), may hold values from -8 to 8
- prompt_ids: int32 [2048], P('loop'), may hold values from 0 to 3, never falling along the last dimension, each value on 1 to 1024 neighbouring positions
- out_weight: bfloat16 [4096, 4096], P('tp'), may hold values from -5 to 5
Outputs:
- mixed: bfloat16 [2048, 4096], P('loop', 'tp')
Inputs may be any that keep to these rules, and one draw needn't show every extreme that they name: `prompt_ids`: prompt numbers never fall along the tokens; each prompt holds 1 to 1024 tokens and one holds exactly 1024.
All inputs are finite; a program needn't handle non-finite values.
Results may differ from a plain program's by a relative error of at most 0.018.
Values may be sent and summed in bfloat16 or wider, within the bound.
A program may use at most 64 MiB of HBM per device.

v0:
```python
import math

import jax
import jax.numpy as jnp
from jax import lax
from jax.sharding import PartitionSpec as P

HD = 128


masked_score = -1e30


def from_behind(value, axis, steps):
    count = lax.axis_size(axis)
    first, last = (max(0, -steps), min(count, count - steps))
    return lax.ppermute(value, axis, [(source, source + steps) for source in range(first, last)])


def per_device(queries, key_values, prompt_ids, out_weight):
    tok_rows = queries.shape[0]
    head_dim = HD
    kv_heads = key_values.shape[1] // (2 * head_dim)
    per_group = queries.shape[1] // (kv_heads * head_dim)
    scaler = 1.0 / math.sqrt(head_dim)
    reach = min(8, lax.axis_size("loop") // 2)
    group_size = max(1, -(-512 // tok_rows))
    query_pos = lax.axis_index("loop") * tok_rows + jnp.arange(tok_rows, dtype=jnp.int32)
    query_heads = queries.reshape(tok_rows, kv_heads, per_group, head_dim)

    def absorb(state_now, pending):
        kv_block = jnp.concatenate([item[0] for item in pending], axis=0)
        id_block = jnp.concatenate([item[1] for item in pending], axis=0)
        key_pos = jnp.concatenate([item[2] for item in pending], axis=0)
        allowed = (
            (prompt_ids[:, None] == id_block[None, :])
            & (key_pos[None, :] <= query_pos[:, None])
            & (key_pos[None, :] >= 0)
        )
        run_max, run_sum, run_acc = state_now
        paired = kv_block.reshape(kv_block.shape[0], kv_heads, 2, head_dim)
        key_rows = paired[:, :, 0, :]
        value_rows = paired[:, :, 1, :]
        scores = (
            jnp.einsum("qhgd,khd->hgqk", query_heads, key_rows, preferred_element_type=jnp.float32)
            * scaler
        )
        scores = jnp.where(allowed, scores, masked_score)
        new_max = jnp.maximum(run_max, jnp.max(scores, axis=-1))
        probs = jnp.where(allowed, jnp.exp(scores - new_max[..., None]), 0.0)
        rescale = jnp.exp(run_max - new_max)
        new_sum = run_sum * rescale + jnp.sum(probs, axis=-1)
        added = jnp.einsum(
            "hgqk,khd->hgqd",
            probs.astype(jnp.bfloat16),
            value_rows,
            preferred_element_type=jnp.float32,
        )
        return (new_max, new_sum, run_acc * rescale[..., None] + added)

    state_now = (
        jnp.full((kv_heads, per_group, tok_rows), masked_score, jnp.float32),
        jnp.zeros((kv_heads, per_group, tok_rows), jnp.float32),
        jnp.zeros((kv_heads, per_group, tok_rows, head_dim), jnp.float32),
    )
    pending = [(key_values, prompt_ids, query_pos)]
    for hop_count in range(1, reach + 1):
        moved_kv, moved_ids = from_behind((key_values, prompt_ids), "loop", hop_count)
        pending.append((moved_kv, moved_ids, query_pos - hop_count * tok_rows))
        if len(pending) >= group_size:
            state_now = absorb(state_now, pending)
            pending = []
    state_now = absorb(state_now, pending)
    run_max, run_sum, run_acc = state_now
    weighted = run_acc / run_sum[..., None]
    attention = (
        jnp.transpose(weighted, (2, 0, 1, 3))
        .reshape(tok_rows, kv_heads * per_group * head_dim)
        .astype(jnp.bfloat16)
    )
    partial_rows = jnp.dot(attention, out_weight, preferred_element_type=jnp.float32)
    return lax.psum_scatter(
        partial_rows.astype(jnp.bfloat16), "tp", scatter_dimension=1, tiled=True
    )


def solution(mesh):
    in_specs = (P("loop", "tp"), P("loop", "tp"), P("loop"), P("tp", None))
    out_specs = P("loop", "tp")
    return jax.shard_map(
        per_device, mesh=mesh, in_specs=in_specs, out_specs=out_specs, check_vma=False
    )
```

profile of v0, /device:TPU:0, one launch (start us, length us, event | category | flops | bytes accessed | tf_op | source)
XLA Modules:
  0.0 96.2 jit_solution(677065872004097795)
XLA Ops:
  6.5 4.4 %collective-permute-start.3 = (s32[256]{0:T(256)}, s32[256]{0:T(256)S(1)}, u32[]{:S(2)}, u32[]{:S(2)}) collective-permute-start(s32[256]{0:T(256)} %param.6), channel_id=1, source_target_pairs={{0,12},{4,16},{8,20},{12,24},{16,28},{1,13},{5,17},{9,21},{13,25},... | collective-permute-start | bytes 3080 | tf_op jit(solution)/shard_map/ppermute | solution.py:17
  11.0 3.4 %collective-permute-start.2 = (s32[256]{0:T(256)}, s32[256]{0:T(256)S(1)}, u32[]{:S(2)}, u32[]{:S(2)}) collective-permute-start(s32[256]{0:T(256)} %param.6), channel_id=1, source_target_pairs={{0,8},{4,12},{8,16},{12,20},{16,24},{20,28},{1,9},{5,13},{9,17},{1... | collective-permute-start | bytes 3080 | tf_op jit(solution)/shard_map/ppermute | solution.py:17
  14.4 2.3 %collective-permute-start = (s32[256]{0:T(256)}, s32[256]{0:T(256)S(1)}, u32[]{:S(2)}, u32[]{:S(2)}) collective-permute-start(s32[256]{0:T(256)} %param.6), channel_id=1, source_target_pairs={{0,4},{4,8},{8,12},{12,16},{16,20},{20,24},{24,28},{1,5},{5,9},{9,... | collective-permute-start | bytes 3080 | tf_op jit(solution)/shard_map/ppermute | solution.py:17
  16.7 1.5 %collective-permute-start.6 = (s32[256]{0:T(256)}, s32[256]{0:T(256)S(1)}, u32[]{:S(2)}, u32[]{:S(2)}) collective-permute-start(s32[256]{0:T(256)} %param.6), channel_id=1, source_target_pairs={{0,16},{4,20},{8,24},{12,28},{1,17},{5,21},{9,25},{13,29},{2,18},{... | collective-permute-start | bytes 3080 | tf_op jit(solution)/shard_map/ppermute | solution.py:17
  18.3 1.0 %copy.15 = bf16[256,256]{0,1:T(8,128)(2,1)S(1)} copy(bf16[256,256]{1,0:T(8,128)(2,1)} %param.5) | data formatting | bytes 262144 | tf_op args[1]
  19.3 1.3 %collective-permute-start.7 = (bf16[256,256]{0,1:T(8,128)(2,1)S(1)}, bf16[256,256]{0,1:T(8,128)(2,1)S(1)}, u32[]{:S(2)}, u32[]{:S(2)}) collective-permute-start(bf16[256,256]{0,1:T(8,128)(2,1)S(1)} %copy.15), channel_id=1, source_target_pairs={{0,16},{4,20},{8,24},{12,28},{1,17},{5,21},{9,25},{13,29},{2,18},{... | collective-permute-start | bytes 393224 | tf_op jit(solution)/shard_map/ppermute | solution.py:17
  20.7 2.5 %collective-permute-start.5 = (bf16[256,256]{0,1:T(8,128)(2,1)S(1)}, bf16[256,256]{0,1:T(8,128)(2,1)S(1)}, u32[]{:S(2)}, u32[]{:S(2)}) collective-permute-start(bf16[256,256]{0,1:T(8,128)(2,1)S(1)} %copy.15), channel_id=1, source_target_pairs={{0,12},{4,16},{8,20},{12,24},{16,28},{1,13},{5,17},{9,21},{13,25},... | collective-permute-start | bytes 393224 | tf_op jit(solution)/shard_map/ppermute | solution.py:17
  23.2 0.7 pad_add_fusion
  23.9 1.6 %collective-permute-start.4 = (bf16[256,256]{0,1:T(8,128)(2,1)S(1)}, bf16[256,256]{0,1:T(8,128)(2,1)S(1)}, u32[]{:S(2)}, u32[]{:S(2)}) collective-permute-start(bf16[256,256]{0,1:T(8,128)(2,1)S(1)} %copy.15), channel_id=1, source_target_pairs={{0,8},{4,12},{8,16},{12,20},{16,24},{20,28},{1,9},{5,13},{9,17},{1... | collective-permute-start | bytes 393224 | tf_op jit(solution)/shard_map/ppermute | solution.py:17
  25.5 2.4 %collective-permute-start.1 = (bf16[256,256]{0,1:T(8,128)(2,1)S(1)}, bf16[256,256]{0,1:T(8,128)(2,1)S(1)}, u32[]{:S(2)}, u32[]{:S(2)}) collective-permute-start(bf16[256,256]{0,1:T(8,128)(2,1)S(1)} %copy.15), channel_id=1, source_target_pairs={{0,4},{4,8},{8,12},{12,16},{16,20},{20,24},{24,28},{1,5},{5,9},{9,... | collective-permute-start | bytes 393224 | tf_op jit(solution)/shard_map/ppermute | solution.py:17
  27.8 1.3 %and_and_fusion = (pred[256,512]{0,1:T(8,128)(4,1)S(1)}, pred[256,512]{0,1:T(8,128)(4,1)S(1)}) fusion(s32[256]{0:T(256)S(1)} %get-tuple-element.20, s32[256]{0:T(256)} %param.6, s32[512]{0:T(512)S(1)} %pad_add_fusion.3, s32[512]{0:T(512)S(1)} %pad_add_fusion.2, pred[512]{0:T(512)(128)(4,1)S(1)} %broadcast_compare_fusion, ...), kind=kLoop, calls=%fused_computation.41 | loop fusion | flops 1048576 | bytes 273408 | tf_op jit(solution)/shard_map/and | solution.py:36
  29.2 0.8 and_and_fusion.2
  30.1 0.9 fusion.1
  31.0 0.5 fusion.14
  31.5 0.9 fusion
  32.4 1.0 %fusion.2 = f32[8,256]{1,0:T(8,128)S(1)} fusion(f32[512,256,8]{1,0,2:T(8,128)S(1)} %get-tuple-element.19, f32[8,256]{1,0:T(8,128)S(1)} %get-tuple-element.11, pred[256,512]{0,1:T(8,128)(4,1)S(1)} %get-tuple-element.13), kind=kLoop, calls=%fused_computation.7 | loop fusion | flops 5240832 | bytes 4341760 | tf_op jit(solution)/shard_map/reduce_sum | solution.py:52
  33.5 0.5 fusion.15
  34.0 1.0 %fusion.4 = f32[8,256]{1,0:T(8,128)S(1)} fusion(f32[512,256,8]{1,0,2:T(8,128)S(1)} %get-tuple-element.17, f32[8,256]{1,0:T(8,128)S(1)} %get-tuple-element.9, pred[256,512]{0,1:T(8,128)(4,1)S(1)} %get-tuple-element.12), kind=kLoop, calls=%fused_computation.9 | loop fusion | flops 5240832 | bytes 4341760 | tf_op jit(solution)/shard_map/reduce_sum | solution.py:52
  35.0 1.3 %fusion.27 = f32[8,256,128]{1,2,0:T(8,128)S(1)} fusion(f32[512,256,8]{1,0,2:T(8,128)S(1)} %get-tuple-element.19, f32[8,256]{1,0:T(8,128)S(1)} %get-tuple-element.11, pred[256,512]{0,1:T(8,128)(4,1)S(1)} %get-tuple-element.13, f32[8,256]{1,0:T(8,128)S(1)} %get-tuple-element.7, f32[8,256]{1,0:T(8,128)S(1)} %get-tuple-element.10, ...), kind=kOutput, calls=%fused_computation.27 | convolution fusion | flops 274202624 | bytes 5529600 | tf_op jit(solution)/shard_map/hgqk,khd->hgqd/dot_general | solution.py:53
  36.4 1.3 %fusion.21 = f32[8,256,128]{1,2,0:T(8,128)S(1)} fusion(f32[8,256,128]{1,2,0:T(8,128)S(1)} %fusion.27, f32[512,256,8]{1,0,2:T(8,128)S(1)} %get-tuple-element.17, f32[8,256]{1,0:T(8,128)S(1)} %get-tuple-element.9, pred[256,512]{0,1:T(8,128)(4,1)S(1)} %get-tuple-element.12, f32[8,256]{1,0:T(8,128)S(1)} %get-tuple-element.6, ...), kind=kOutput, calls=%fused_computation.25 | convolution fusion | flops 274202624 | bytes 6569984 | tf_op jit(solution)/shard_map/hgqk,khd->hgqd/dot_general | solution.py:53
  37.7 0.7 fusion.30
  38.4 0.3 slice-done.1
  38.8 3.9 %convolution_convert_fusion = bf16[256,4096]{1,0:T(8,128)(2,1)} fusion(bf16[256,1024]{0,1:T(8,128)(2,1)S(1)} %bitcast.144, bf16[1024,4096]{1,0:T(8,128)(2,1)S(1)} %bitcast.143), kind=kOutput, calls=%fused_computation | convolution fusion | flops 2148532224 | bytes 11010048 | tf_op jit(solution)/shard_map/dot_general | solution.py:81
  42.6 46.7 %reduce-scatter.2.cloned.1.call-done = bf16[256,1024]{1,0:T(8,128)(2,1)} async-done(((bf16[256,4096]{1,0:T(8,128)(2,1)}), bf16[256,1024]{1,0:T(8,128)(2,1)}) %reduce-scatter.2.cloned.1.call-update) | async-done | bytes 524304 | tf_op jit(solution)/shard_map/reduce_scatter | solution.py:82
  (29 shorter events, 0.2 us)
Async XLA Ops:
  6.5 23.6 %copy-start = (bf16[256,1024]{1,0:T(8,128)(2,1)S(1)}, bf16[256,1024]{1,0:T(8,128)(2,1)}, u32[]{:S(2)}) copy-start(bf16[256,1024]{1,0:T(8,128)(2,1)} %param.4) | copy-start | bytes 1572868
  6.5 82.8 %reduce-scatter.2.cloned.1.call-start = ((), (), s32[]{:S(2)}) async-start(), calls=%async_computation.1 | async-start | bytes 2621440 | tf_op jit(solution)/shard_map/reduce_scatter | solution.py:82
  6.5 17.3 %collective-permute-start.3 = (s32[256]{0:T(256)}, s32[256]{0:T(256)S(1)}, u32[]{:S(2)}, u32[]{:S(2)}) collective-permute-start(s32[256]{0:T(256)} %param.6), channel_id=1, source_target_pairs={{0,12},{4,16},{8,20},{12,24},{16,28},{1,13},{5,17},{9,21},{13,25},... | collective-permute-start | bytes 3080 | tf_op jit(solution)/shard_map/ppermute | solution.py:17
  11.0 14.5 %collective-permute-start.2 = (s32[256]{0:T(256)}, s32[256]{0:T(256)S(1)}, u32[]{:S(2)}, u32[]{:S(2)}) collective-permute-start(s32[256]{0:T(256)} %param.6), channel_id=1, source_target_pairs={{0,8},{4,12},{8,16},{12,20},{16,24},{20,28},{1,9},{5,13},{9,17},{1... | collective-permute-start | bytes 3080 | tf_op jit(solution)/shard_map/ppermute | solution.py:17
  14.4 6.3 %collective-permute-start = (s32[256]{0:T(256)}, s32[256]{0:T(256)S(1)}, u32[]{:S(2)}, u32[]{:S(2)}) collective-permute-start(s32[256]{0:T(256)} %param.6), channel_id=1, source_target_pairs={{0,4},{4,8},{8,12},{12,16},{16,20},{20,24},{24,28},{1,5},{5,9},{9,... | collective-permute-start | bytes 3080 | tf_op jit(solution)/shard_map/ppermute | solution.py:17
  16.7 12.5 %collective-permute-start.6 = (s32[256]{0:T(256)}, s32[256]{0:T(256)S(1)}, u32[]{:S(2)}, u32[]{:S(2)}) collective-permute-start(s32[256]{0:T(256)} %param.6), channel_id=1, source_target_pairs={{0,16},{4,20},{8,24},{12,28},{1,17},{5,21},{9,25},{13,29},{2,18},{... | collective-permute-start | bytes 3080 | tf_op jit(solution)/shard_map/ppermute | solution.py:17
  19.3 11.7 %collective-permute-start.7 = (bf16[256,256]{0,1:T(8,128)(2,1)S(1)}, bf16[256,256]{0,1:T(8,128)(2,1)S(1)}, u32[]{:S(2)}, u32[]{:S(2)}) collective-permute-start(bf16[256,256]{0,1:T(8,128)(2,1)S(1)} %copy.15), channel_id=1, source_target_pairs={{0,16},{4,20},{8,24},{12,28},{1,17},{5,21},{9,25},{13,29},{2,18},{... | collective-permute-start | bytes 393224 | tf_op jit(solution)/shard_map/ppermute | solution.py:17
  20.7 9.4 %collective-permute-start.5 = (bf16[256,256]{0,1:T(8,128)(2,1)S(1)}, bf16[256,256]{0,1:T(8,128)(2,1)S(1)}, u32[]{:S(2)}, u32[]{:S(2)}) collective-permute-start(bf16[256,256]{0,1:T(8,128)(2,1)S(1)} %copy.15), channel_id=1, source_target_pairs={{0,12},{4,16},{8,20},{12,24},{16,28},{1,13},{5,17},{9,21},{13,25},... | collective-permute-start | bytes 393224 | tf_op jit(solution)/shard_map/ppermute | solution.py:17
  23.9 6.2 %collective-permute-start.4 = (bf16[256,256]{0,1:T(8,128)(2,1)S(1)}, bf16[256,256]{0,1:T(8,128)(2,1)S(1)}, u32[]{:S(2)}, u32[]{:S(2)}) collective-permute-start(bf16[256,256]{0,1:T(8,128)(2,1)S(1)} %copy.15), channel_id=1, source_target_pairs={{0,8},{4,12},{8,16},{12,20},{16,24},{20,28},{1,9},{5,13},{9,17},{1... | collective-permute-start | bytes 393224 | tf_op jit(solution)/shard_map/ppermute | solution.py:17
  25.5 6.1 %collective-permute-start.1 = (bf16[256,256]{0,1:T(8,128)(2,1)S(1)}, bf16[256,256]{0,1:T(8,128)(2,1)S(1)}, u32[]{:S(2)}, u32[]{:S(2)}) collective-permute-start(bf16[256,256]{0,1:T(8,128)(2,1)S(1)} %copy.15), channel_id=1, source_target_pairs={{0,4},{4,8},{8,12},{12,16},{16,20},{20,24},{24,28},{1,5},{5,9},{9,... | collective-permute-start | bytes 393224 | tf_op jit(solution)/shard_map/ppermute | solution.py:17
  35.0 3.4 %slice-start = ((s8[8388608]{0:T(1024)(128)(4,1)}), s8[4194304]{0:T(1024)(128)(4,1)S(1)}, s32[]{:S(2)}) async-start(s8[8388608]{0:T(1024)(128)(4,1)} %bitcast.142), calls=%async_computation.2 | async-start | bytes 8388608
  36.4 2.4 %slice-start.1 = ((s8[8388608]{0:T(1024)(128)(4,1)}), s8[4194304]{0:T(1024)(128)(4,1)S(1)}, s32[]{:S(2)}) async-start(s8[8388608]{0:T(1024)(128)(4,1)} %bitcast.142), calls=%async_computation.3 | async-start | bytes 8388608
Sparse Core Ops, SparseCore 0:
  42.8 46.5 reduce-scatter.1
where the time goes:
time: 96.5 us; the launch traced here: 96.2 us
  waiting for transfers between devices  46.7 us (48%)
  starting transfers between devices  19.4 us (20%)
  between operations  13.7 us (14%)
  matrix products  9.43 us (10%)
  other arithmetic  5.56 us (6%)
  local copies, waits for them, and re-layouts  1.35 us (1%)
    reduce_scatter x1, waiting for transfers between devices, per_device(): lax.psum_scatter(partial_rows.astype(jnp.bfloat16), 'tp', scatter_dimensi...  46.7 us
    ppermute x8, starting transfers between devices, from_behind(): lax.ppermute(value, axis, [(source, source + steps) for source in range(f...  19.4 us
    dot_general x1, matrix products, per_device(): jnp.dot(attention, out_weight, preferred_element_type=jnp.float32)  3.86 us
    dot_general x3, matrix products, absorb(): jnp.einsum('hgqk,khd->hgqd', probs.astype(jnp.bfloat16), value_rows, pref...  3.34 us
    reduce_sum x3, other arithmetic, absorb(): new_sum = run_sum * rescale + jnp.sum(probs, axis=-1)  2.55 us
    dot_general x3, matrix products, absorb(): jnp.einsum('qhgd,khd->hgqk', query_heads, key_rows, preferred_element_typ...  2.24 us
    and x2, other arithmetic, absorb(): (prompt_ids[:, None] == id_block[None, :]) & (key_pos[None, :] <= query_p...  2.18 us
  transfers between devices with their start and end apart: 9, of which 1 were waited for; matrix products, arithmetic and copies ran while one was open for 6% of the time, Pallas kernels for 0%

commit v1 on v0

v1 whole, which is shorter than its diff:
```python
import functools
import math

import jax
import jax.numpy as jnp
from jax import lax
from jax.experimental import pallas as pl
from jax.experimental.pallas import tpu as pltpu
from jax.sharding import PartitionSpec as P

HD = 128
BLOCKED = -1e30
ROWS = 64
STACK = 2
MESH = pl.DeviceIdType.MESH


def kernel(n_loop, n_tp, reach, q_hbm, kv_hbm, ids_ref, w_hbm, out_ref,
           q_ref, kv_buf, v_buf, id_buf, q_col, bias, attn, w_ref, part, recv_r, recv_l,
           load_sem, kv_send, kv_recv, id_send, id_recv, send_sem, r_sem, l_sem):
    tok = q_ref.shape[0]
    heads = q_ref.shape[1] // HD
    width = part.shape[2]
    blocks = tok // ROWS
    far_last = reach * tok
    scale = math.log2(math.e) / math.sqrt(HD)
    i = lax.axis_index("loop")
    z = lax.axis_index("tp")

    load_q = pltpu.make_async_copy(q_hbm, q_ref, load_sem.at[0])
    load_kv = pltpu.make_async_copy(kv_hbm, kv_buf.at[reach], load_sem.at[1])
    load_w = pltpu.make_async_copy(w_hbm, w_ref, load_sem.at[2])
    load_kv.start()
    load_q.start()
    load_w.start()

    def kv_copy(k):
        return pltpu.make_async_remote_copy(
            src_ref=kv_hbm, dst_ref=kv_buf.at[reach - k], send_sem=kv_send.at[k - 1],
            recv_sem=kv_recv.at[k - 1], device_id=(i + k, z), device_id_type=MESH)

    def id_copy(k):
        return pltpu.make_async_remote_copy(
            src_ref=ids_ref, dst_ref=id_buf.at[reach - k], send_sem=id_send.at[k - 1],
            recv_sem=id_recv.at[k - 1], device_id=(i + k, z), device_id_type=MESH)

    def right_copy(c, b):
        rows = pl.ds(pl.multiple_of(b * ROWS, ROWS), ROWS)
        return pltpu.make_async_remote_copy(
            src_ref=part.at[c, rows], dst_ref=recv_r.at[c, rows], send_sem=send_sem.at[c, b],
            recv_sem=r_sem.at[c, b], device_id=(i, z + 1), device_id_type=MESH)

    def left_copy(c, b):
        rows = pl.ds(pl.multiple_of(b * ROWS, ROWS), ROWS)
        return pltpu.make_async_remote_copy(
            src_ref=part.at[c, rows], dst_ref=recv_l.at[c, rows], send_sem=send_sem.at[c, b],
            recv_sem=l_sem.at[c, b], device_id=(i, z - 1), device_id_type=MESH)

    barrier = pltpu.get_barrier_semaphore()
    for k in range(1, reach + 1):
        @pl.when(i + k < n_loop)
        def _():
            pl.semaphore_signal(barrier, inc=1, device_id=(i + k, z), device_id_type=MESH)

        @pl.when(i - k >= 0)
        def _():
            pl.semaphore_signal(barrier, inc=1, device_id=(i - k, z), device_id_type=MESH)

    @pl.when(z > 0)
    def _():
        pl.semaphore_signal(barrier, inc=1, device_id=(i, z - 1), device_id_type=MESH)

    @pl.when(z < n_tp - 1)
    def _():
        pl.semaphore_signal(barrier, inc=1, device_id=(i, z + 1), device_id_type=MESH)

    greeted = (jnp.minimum(i, reach) + jnp.minimum(n_loop - 1 - i, reach)
               + jnp.minimum(z, 1) + jnp.minimum(n_tp - 1 - z, 1))
    pl.semaphore_wait(barrier, greeted)

    for k in range(1, reach + 1):
        @pl.when(i + k < n_loop)
        def _():
            id_copy(k).start()
            kv_copy(k).start()

    for k in range(1, reach + 1):
        @pl.when(i < k)
        def _():
            kv_buf[reach - k] = jnp.zeros(kv_buf.shape[1:], kv_buf.dtype)
            id_buf[reach - k] = jnp.full(id_buf.shape[1:], -1, id_buf.dtype)
    id_buf[reach] = ids_ref[...]
    own_ids = ids_ref[...].astype(jnp.float32)
    square = (tok, tok)
    q_col[...] = jnp.max(
        jnp.where(lax.broadcasted_iota(jnp.int32, square, 0) == lax.broadcasted_iota(jnp.int32, square, 1),
                  jnp.broadcast_to(own_ids, square), -1.0), axis=1, keepdims=True)
    v_buf[:, HD:] = jnp.ones((v_buf.shape[0], HD), v_buf.dtype)
    load_kv.wait()
    load_q.wait()
    load_w.wait()
    for k in range(1, reach + 1):
        @pl.when(i >= k)
        def _():
            id_copy(k).wait_recv()
            kv_copy(k).wait_recv()
    for s in range(reach + 1):
        v_buf[s * tok:(s + 1) * tok, :HD] = kv_buf[s, :, HD:]

    def compute(b):
        rows = pl.ds(pl.multiple_of(b * ROWS, ROWS), ROWS)
        q_ids = q_col[rows, :]
        shape = (ROWS, tok)
        lower = (lax.broadcasted_iota(jnp.int32, shape, 1)
                 <= lax.broadcasted_iota(jnp.int32, shape, 0) + b * ROWS)
        key_ids = [jnp.broadcast_to(id_buf[s].astype(jnp.float32), shape) for s in range(reach + 1)]
        shared = jnp.where(lower, key_ids[reach], key_ids[0])
        for s, ids in enumerate([shared] + key_ids[1:reach]):
            bias[:, s * tok:(s + 1) * tok] = jnp.where(ids == q_ids, 0.0, BLOCKED)
        keys = kv_buf[:, :, :HD].reshape((reach + 1) * tok, HD)
        for h in range(0, heads, STACK):
            q = jnp.concatenate([q_ref[rows, (h + j) * HD:(h + j + 1) * HD] for j in range(STACK)], axis=0)
            s = lax.dot_general(q, keys, (((1,), (1,)), ((), ())), preferred_element_type=jnp.float32)
            s = s.reshape(STACK, ROWS, (reach + 1) * tok)
            s = jnp.concatenate(
                [jnp.where(lower[None], s[:, :, far_last:], s[:, :, :tok]), s[:, :, tok:far_last]], axis=2)
            s = s * scale + bias[...][None]
            p = jnp.exp2(s - jnp.max(s, axis=2, keepdims=True))
            first = p[:, :, :tok]
            p = jnp.concatenate(
                [jnp.where(lower[None], 0.0, first), p[:, :, tok:], jnp.where(lower[None], first, 0.0)], axis=2)
            p = p.reshape(STACK * ROWS, (reach + 1) * tok).astype(jnp.bfloat16)
            o = jnp.dot(p, v_buf[...], preferred_element_type=jnp.float32)
            o = (o[:, :HD] / o[:, HD:]).astype(jnp.bfloat16)
            for j in range(STACK):
                attn[:, (h + j) * HD:(h + j + 1) * HD] = o[j * ROWS:(j + 1) * ROWS]
        order = []
        for c in range((n_tp + 1) // 2):
            order += [n_tp - 1 - c, c] if c != n_tp - 1 - c else [c]
        for c in order:
            part[c, rows, :] = jnp.dot(
                attn[...], w_ref[:, c * width:(c + 1) * width],
                preferred_element_type=jnp.float32).astype(jnp.bfloat16)
            if c >= 2:
                @pl.when(z == 0)
                def _():
                    right_copy(c, b).start()
            if c < n_tp - 2:
                @pl.when(z == n_tp - 1)
                def _():
                    left_copy(c, b).start()

    def forward_right(b):
        rows = pl.ds(pl.multiple_of(b * ROWS, ROWS), ROWS)
        for c in range(n_tp - 1, 1, -1):
            @pl.when(c > z)
            def _():
                copy = right_copy(c, b)
                copy.wait_recv()
                part[c, rows, :] = (part[c, rows, :].astype(jnp.float32)
                                    + recv_r[c, rows, :].astype(jnp.float32)).astype(jnp.bfloat16)
                copy.start()

    def forward_left(b):
        rows = pl.ds(pl.multiple_of(b * ROWS, ROWS), ROWS)
        for c in range(n_tp - 2):
            @pl.when(c < z)
            def _():
                copy = left_copy(c, b)
                copy.wait_recv()
                part[c, rows, :] = (part[c, rows, :].astype(jnp.float32)
                                    + recv_l[c, rows, :].astype(jnp.float32)).astype(jnp.bfloat16)
                copy.start()

    low_half = z < n_tp // 2
    middle = jnp.logical_and(z > 0, z < n_tp - 1)

    def step(b, carry):
        @pl.when(b < blocks)
        def _():
            compute(b)

        right_b = b - jnp.where(low_half, 1, 2)
        left_b = b - jnp.where(low_half, 2, 1)

        @pl.when(middle & (right_b >= 0) & (right_b < blocks))
        def _():
            forward_right(right_b)

        @pl.when(middle & (left_b >= 0) & (left_b < blocks))
        def _():
            forward_left(left_b)
        return carry

    lax.fori_loop(0, blocks + 2, step, 0)

    @pl.when(z == 0)
    def _():
        for b in range(blocks):
            for c in range(n_tp - 1, 1, -1):
                right_copy(c, b).wait_send()
            if b == blocks - 2:
                for late in range(blocks):
                    right_copy(1, late).start()

    @pl.when(z == n_tp - 1)
    def _():
        for b in range(blocks):
            for c in range(n_tp - 2):
                left_copy(c, b).wait_send()
            if b == blocks - 2:
                for late in range(blocks):
                    left_copy(n_tp - 2, late).start()

    def finish(b, carry):
        rows = pl.ds(pl.multiple_of(b * ROWS, ROWS), ROWS)

        @pl.when(z == 0)
        def _():
            left_copy(z, b).wait_recv()
            out_ref[rows, :] = (part[z, rows, :].astype(jnp.float32)
                                + recv_l[z, rows, :].astype(jnp.float32)).astype(out_ref.dtype)

        @pl.when(z == n_tp - 1)
        def _():
            right_copy(z, b).wait_recv()
            out_ref[rows, :] = (part[z, rows, :].astype(jnp.float32)
                                + recv_r[z, rows, :].astype(jnp.float32)).astype(out_ref.dtype)

        @pl.when(middle)
        def _():
            right_copy(z, b).wait_recv()
            left_copy(z, b).wait_recv()
            out_ref[rows, :] = (part[z, rows, :].astype(jnp.float32)
                                + recv_r[z, rows, :].astype(jnp.float32)
                                + recv_l[z, rows, :].astype(jnp.float32)).astype(out_ref.dtype)
        return carry

    lax.fori_loop(0, blocks, finish, 0)

    for k in range(1, reach + 1):
        @pl.when(i + k < n_loop)
        def _():
            id_copy(k).wait_send()
            kv_copy(k).wait_send()

    def drain(b, carry):
        @pl.when(z == 0)
        def _():
            right_copy(1, b).wait_send()

        @pl.when(z == n_tp - 1)
        def _():
            left_copy(n_tp - 2, b).wait_send()

        for c in range(n_tp):
            @pl.when(middle & (c > z))
            def _():
                right_copy(c, b).wait_send()

            @pl.when(middle & (c < z))
            def _():
                left_copy(c, b).wait_send()
        return carry

    lax.fori_loop(0, blocks, drain, 0)


def per_device(queries, key_values, prompt_ids, out_weight):
    n_loop, n_tp = lax.axis_size("loop"), lax.axis_size("tp")
    tok, q_cols = queries.shape
    depth, d_out = out_weight.shape
    width = d_out // n_tp
    reach = min(8, n_loop // 2)
    blocks = tok // ROWS
    vmem = pltpu.VMEM
    dma = pltpu.SemaphoreType.DMA
    any_spec = pl.BlockSpec(memory_space=pl.ANY)
    vmem_spec = pl.BlockSpec(memory_space=pltpu.VMEM)
    return pl.pallas_call(
        functools.partial(kernel, n_loop, n_tp, reach),
        out_shape=jax.ShapeDtypeStruct((tok, width), jnp.bfloat16),
        in_specs=[any_spec, any_spec, vmem_spec, any_spec],
        out_specs=vmem_spec,
        scratch_shapes=[
            vmem((tok, q_cols), jnp.bfloat16),
            vmem((reach + 1, tok, 2 * HD), jnp.bfloat16),
            vmem(((reach + 1) * tok, 2 * HD), jnp.bfloat16),
            vmem((reach + 1, 1, tok), jnp.int32),
            vmem((tok, 1), jnp.float32),
            vmem((ROWS, reach * tok), jnp.float32),
            vmem((ROWS, q_cols), jnp.bfloat16),
            vmem((depth, d_out), jnp.bfloat16),
            vmem((n_tp, tok, width), jnp.bfloat16),
            vmem((n_tp, tok, width), jnp.bfloat16),
            vmem((n_tp, tok, width), jnp.bfloat16),
            dma((3,)), dma((reach,)), dma((reach,)), dma((reach,)), dma((reach,)),
            dma((n_tp, blocks)), dma((n_tp, blocks)), dma((n_tp, blocks)),
        ],
        compiler_params=pltpu.CompilerParams(
            collective_id=0, has_side_effects=True, vmem_limit_bytes=56 * 1024 * 1024),
        cost_estimate=pl.CostEstimate(flops=3_500_000_000, bytes_accessed=10_000_000, transcendentals=2_000_000),
    )(queries, key_values, prompt_ids.reshape(1, tok), out_weight)


def solution(mesh):
    in_specs = (P("loop", "tp"), P("loop", "tp"), P("loop"), P("tp", None))
    out_specs = P("loop", "tp")
    return jax.shard_map(
        per_device, mesh=mesh, in_specs=in_specs, out_specs=out_specs, check_vma=False
    )
```

time: 96.5 us -> 55.9 us (0.58)
  the two profiles are of different devices: /device:TPU:0 before, /device:TPU:21 now
where the time goes in v1:
time: 55.9 us; the launch traced here: 55.8 us
  Pallas kernels  53.9 us (96%)
  local copies, waits for them, and re-layouts  1.87 us (3%)
    pallas_call x1, Pallas kernels, per_device(): pl.pallas_call(functools.partial(kernel, n_loop, n_tp, reach), out_shape=...  53.9 us
    unnamed x1, local copies, waits for them, and re-layouts  1.87 us

profile of v1, /device:TPU:21, one launch (start us, length us, event | category | flops | bytes accessed | tf_op | source)
XLA Modules:
  0.0 55.8 jit_solution(7538693347615964962)
XLA Ops:
  0.0 53.9 %shard_map.46 = bf16[256,1024]{1,0:T(8,128)(2,1)} custom-call(bf16[256,1024]{1,0:T(8,128)(2,1)} %q_hbm.1, bf16[256,256]{1,0:T(8,128)(2,1)} %kv_hbm.1, s32[1,256]{1,0:T(1,128)} %bitcast.1, bf16[1024,4096]{1,0:T(8,128)(2,1)} %w_hbm.1), custom_call_target="tpu_custom_call" | custom-call | flops 3500000000 | bytes 10000000 | tf_op jit(solution)/shard_map/pallas_call | solution.py:280
  53.9 1.9 %copy.6 = bf16[256,1024]{1,0:T(8,128)(2,1)} copy(bf16[256,1024]{1,0:T(8,128)(2,1)} %shard_map.46) | data formatting | bytes 1048576

commit v2 on v1

--- a/solution.py
+++ b/solution.py
@@ -15,7 +15,7 @@
 MESH = pl.DeviceIdType.MESH
 
 
-def kernel(n_loop, n_tp, reach, q_hbm, kv_hbm, ids_ref, w_hbm, out_ref,
+def kernel(n_loop, n_tp, reach, q_hbm, kv_hbm, ids_ref, w_hbm, out_ref, more_ref,
            q_ref, kv_buf, v_buf, id_buf, q_col, bias, attn, w_ref, part, recv_r, recv_l,
            load_sem, kv_send, kv_recv, id_send, id_recv, send_sem, r_sem, l_sem):
     tok = q_ref.shape[0]
@@ -34,15 +34,34 @@
     load_q.start()
     load_w.start()
 
-    def kv_copy(k):
-        return pltpu.make_async_remote_copy(
-            src_ref=kv_hbm, dst_ref=kv_buf.at[reach - k], send_sem=kv_send.at[k - 1],
-            recv_sem=kv_recv.at[k - 1], device_id=(i + k, z), device_id_type=MESH)
-
-    def id_copy(k):
-        return pltpu.make_async_remote_copy(
-            src_ref=ids_ref, dst_ref=id_buf.at[reach - k], send_sem=id_send.at[k - 1],
-            recv_sem=id_recv.at[k - 1], device_id=(i + k, z), device_id_type=MESH)
+    core = lax.rem(i, 2)
+    hops = reach // 2
+
+    def chip_copies(d):
+        slot = reach - 2 * d
+        return [
+            pltpu.make_async_remote_copy(
+                src_ref=source, dst_ref=target.at[slot], send_sem=sends.at[d - 1],
+                recv_sem=arrivals.at[2 * d - 1], device_id=(i + 2 * d, z), device_id_type=MESH)
+            for source, target, sends, arrivals in (
+                (ids_ref, id_buf, id_send, id_recv), (kv_hbm, kv_buf, kv_send, kv_recv))]
+
+    def up_copies(d):
+        return [
+            pltpu.make_async_remote_copy(
+                src_ref=source if d == 0 else target.at[reach - 2 * d], dst_ref=target.at[reach - 2 * d - 1],
+                send_sem=sends.at[hops + d], recv_sem=arrivals.at[2 * d],
+                device_id=(i + 1, z), device_id_type=MESH)
+            for source, target, sends, arrivals in (
+                (ids_ref, id_buf, id_send, id_recv), (kv_hbm, kv_buf, kv_send, kv_recv))]
+
+    def down_copies(d):
+        return [
+            pltpu.make_async_remote_copy(
+                src_ref=target.at[reach - 2 * d], dst_ref=target.at[reach - 2 * d + 1],
+                send_sem=sends.at[hops + d - 1], recv_sem=arrivals.at[2 * d - 2],
+                device_id=(i - 1, z), device_id_type=MESH)
+            for target, sends, arrivals in ((id_buf, id_send, id_recv), (kv_buf, kv_send, kv_recv))]
 
     def right_copy(c, b):
         rows = pl.ds(pl.multiple_of(b * ROWS, ROWS), ROWS)
@@ -57,14 +76,15 @@
             recv_sem=l_sem.at[c, b], device_id=(i, z - 1), device_id_type=MESH)
 
     barrier = pltpu.get_barrier_semaphore()
-    for k in range(1, reach + 1):
-        @pl.when(i + k < n_loop)
-        def _():
-            pl.semaphore_signal(barrier, inc=1, device_id=(i + k, z), device_id_type=MESH)
-
-        @pl.when(i - k >= 0)
-        def _():
-            pl.semaphore_signal(barrier, inc=1, device_id=(i - k, z), device_id_type=MESH)
+    pl.semaphore_signal(barrier, inc=1, device_id=(i + 1 - 2 * core, z), device_id_type=MESH)
+    for d in range(1, hops + 1):
+        @pl.when(i + 2 * d < n_loop)
+        def _():
+            pl.semaphore_signal(barrier, inc=1, device_id=(i + 2 * d, z), device_id_type=MESH)
+
+        @pl.when(i - 2 * d >= 0)
+        def _():
+            pl.semaphore_signal(barrier, inc=1, device_id=(i - 2 * d, z), device_id_type=MESH)
 
     @pl.when(z > 0)
     def _():
@@ -74,15 +94,21 @@
     def _():
         pl.semaphore_signal(barrier, inc=1, device_id=(i, z + 1), device_id_type=MESH)
 
-    greeted = (jnp.minimum(i, reach) + jnp.minimum(n_loop - 1 - i, reach)
+    chip = i // 2
+    greeted = (1 + jnp.minimum(chip, hops) + jnp.minimum(n_loop // 2 - 1 - chip, hops)
                + jnp.minimum(z, 1) + jnp.minimum(n_tp - 1 - z, 1))
     pl.semaphore_wait(barrier, greeted)
 
-    for k in range(1, reach + 1):
-        @pl.when(i + k < n_loop)
-        def _():
-            id_copy(k).start()
-            kv_copy(k).start()
+    for d in range(1, hops + 1):
+        @pl.when(i + 2 * d < n_loop)
+        def _():
+            for copy in chip_copies(d):
+                copy.start()
+
+    @pl.when(core == 0)
+    def _():
+        for copy in up_copies(0):
+            copy.start()
 
     for k in range(1, reach + 1):
         @pl.when(i < k)
@@ -98,12 +124,32 @@
     v_buf[:, HD:] = jnp.ones((v_buf.shape[0], HD), v_buf.dtype)
     load_kv.wait()
     load_q.wait()
-    load_w.wait()
-    for k in range(1, reach + 1):
-        @pl.when(i >= k)
-        def _():
-            id_copy(k).wait_recv()
-            kv_copy(k).wait_recv()
+    for d in range(1, hops + 1):
+        @pl.when(i >= 2 * d)
+        def _():
+            for copy in chip_copies(d):
+                copy.wait_recv()
+
+            @pl.when(core == 1)
+            def _():
+                for copy in down_copies(d):
+                    copy.start()
+
+            if d < hops:
+                @pl.when(core == 0)
+                def _():
+                    for copy in up_copies(d):
+                        copy.start()
+    for d in range(1, hops + 1):
+        @pl.when((core == 0) & (i >= 2 * d))
+        def _():
+            for copy in down_copies(d):
+                copy.wait_recv()
+
+        @pl.when((core == 1) & (i >= 2 * d - 1))
+        def _():
+            for copy in up_copies(d - 1):
+                copy.wait_recv()
     for s in range(reach + 1):
         v_buf[s * tok:(s + 1) * tok, :HD] = kv_buf[s, :, HD:]
 
@@ -134,6 +180,10 @@
             o = (o[:, :HD] / o[:, HD:]).astype(jnp.bfloat16)
             for j in range(STACK):
                 attn[:, (h + j) * HD:(h + j + 1) * HD] = o[j * ROWS:(j + 1) * ROWS]
+
+        @pl.when(b == 0)
+        def _():
+            load_w.wait()
         order = []
         for c in range((n_tp + 1) // 2):
             order += [n_tp - 1 - c, c] if c != n_tp - 1 - c else [c]
@@ -218,31 +268,41 @@
         @pl.when(z == 0)
         def _():
             left_copy(z, b).wait_recv()
-            out_ref[rows, :] = (part[z, rows, :].astype(jnp.float32)
-                                + recv_l[z, rows, :].astype(jnp.float32)).astype(out_ref.dtype)
+            out_ref[rows, :] = part[z, rows, :]
+            more_ref[rows, :] = recv_l[z, rows, :]
 
         @pl.when(z == n_tp - 1)
         def _():
             right_copy(z, b).wait_recv()
-            out_ref[rows, :] = (part[z, rows, :].astype(jnp.float32)
-                                + recv_r[z, rows, :].astype(jnp.float32)).astype(out_ref.dtype)
+            out_ref[rows, :] = part[z, rows, :]
+            more_ref[rows, :] = recv_r[z, rows, :]
 
         @pl.when(middle)
         def _():
             right_copy(z, b).wait_recv()
             left_copy(z, b).wait_recv()
-            out_ref[rows, :] = (part[z, rows, :].astype(jnp.float32)
-                                + recv_r[z, rows, :].astype(jnp.float32)
-                                + recv_l[z, rows, :].astype(jnp.float32)).astype(out_ref.dtype)
+            out_ref[rows, :] = part[z, rows, :]
+            more_ref[rows, :] = (recv_r[z, rows, :].astype(jnp.float32)
+                                 + recv_l[z, rows, :].astype(jnp.float32)).astype(out_ref.dtype)
         return carry
 
     lax.fori_loop(0, blocks, finish, 0)
 
-    for k in range(1, reach + 1):
-        @pl.when(i + k < n_loop)
-        def _():
-            id_copy(k).wait_send()
-            kv_copy(k).wait_send()
+    for d in range(1, hops + 1):
+        @pl.when(i + 2 * d < n_loop)
+        def _():
+            for copy in chip_copies(d):
+                copy.wait_send()
+
+        @pl.when((core == 1) & (i >= 2 * d))
+        def _():
+            for copy in down_copies(d):
+                copy.wait_send()
+
+        @pl.when((core == 0) & (i >= 2 * d - 2))
+        def _():
+            for copy in up_copies(d - 1):
+                copy.wait_send()
 
     def drain(b, carry):
         @pl.when(z == 0)
@@ -277,11 +337,11 @@
     dma = pltpu.SemaphoreType.DMA
     any_spec = pl.BlockSpec(memory_space=pl.ANY)
     vmem_spec = pl.BlockSpec(memory_space=pltpu.VMEM)
-    return pl.pallas_call(
+    one, more = pl.pallas_call(
         functools.partial(kernel, n_loop, n_tp, reach),
-        out_shape=jax.ShapeDtypeStruct((tok, width), jnp.bfloat16),
+        out_shape=[jax.ShapeDtypeStruct((tok, width), jnp.bfloat16)] * 2,
         in_specs=[any_spec, any_spec, vmem_spec, any_spec],
-        out_specs=vmem_spec,
+        out_specs=[vmem_spec] * 2,
         scratch_shapes=[
             vmem((tok, q_cols), jnp.bfloat16),
             vmem((reach + 1, tok, 2 * HD), jnp.bfloat16),
@@ -301,6 +361,7 @@
             collective_id=0, has_side_effects=True, vmem_limit_bytes=56 * 1024 * 1024),
         cost_estimate=pl.CostEstimate(flops=3_500_000_000, bytes_accessed=10_000_000, transcendentals=2_000_000),
     )(queries, key_values, prompt_ids.reshape(1, tok), out_weight)
+    return (one.astype(jnp.float32) + more.astype(jnp.float32)).astype(jnp.bfloat16)
 
 
 def solution(mesh):

time: 55.9 us -> 51.1 us (0.914)
  the two profiles are of different devices: /device:TPU:21 before, /device:TPU:20 now
where the time goes in v2:
time: 51.1 us; the launch traced here: 50.9 us
  Pallas kernels  48.7 us (95%)
  other arithmetic  2.19 us (4%)
    pallas_call x1, Pallas kernels, per_device(): pl.pallas_call(functools.partial(kernel, n_loop, n_tp, reach), out_shape=...  48.7 us
    convert_element_type x1, other arithmetic, per_device(): (one.astype(jnp.float32) + more.astype(jnp.float32)).astype(jnp.bfloat16)  2.19 us

profile of v2, /device:TPU:20, one launch (start us, length us, event | category | flops | bytes accessed | tf_op | source)
XLA Modules:
  0.0 50.9 jit_solution(13692196479748268616)
XLA Ops:
  0.0 48.7 %shard_map.46 = (bf16[256,1024]{1,0:T(8,128)(2,1)}, bf16[256,1024]{1,0:T(8,128)(2,1)}) custom-call(bf16[256,1024]{1,0:T(8,128)(2,1)} %q_hbm.1, bf16[256,256]{1,0:T(8,128)(2,1)} %kv_hbm.1, s32[1,256]{1,0:T(1,128)} %bitcast.1, bf16[1024,4096]{1,0:T(8,128)(2,1)} %w_hbm.1), custom_call_target="tpu_custom_call" | custom-call | flops 3500000000 | bytes 10000000 | tf_op jit(solution)/shard_map/pallas_call | solution.py:340
  48.8 2.2 %add_convert_fusion = bf16[256,1024]{1,0:T(8,128)(2,1)} fusion(bf16[256,1024]{1,0:T(8,128)(2,1)} %get-tuple-element.8, bf16[256,1024]{1,0:T(8,128)(2,1)} %get-tuple-element.7), kind=kLoop, calls=%fused_computation | loop fusion | flops 1048576 | bytes 1572864 | tf_op jit(solution)/shard_map/convert_element_type | solution.py:364

commit v3 on v2

--- a/solution.py
+++ b/solution.py
@@ -10,12 +10,12 @@
 
 HD = 128
 BLOCKED = -1e30
-ROWS = 64
-STACK = 2
+ROWS = 32
+STACK = 4
 MESH = pl.DeviceIdType.MESH
 
 
-def kernel(n_loop, n_tp, reach, q_hbm, kv_hbm, ids_ref, w_hbm, out_ref, more_ref,
+def kernel(n_loop, n_tp, reach, q_hbm, kv_hbm, ids_hbm, w_hbm, out_ref,
            q_ref, kv_buf, v_buf, id_buf, q_col, bias, attn, w_ref, part, recv_r, recv_l,
            load_sem, kv_send, kv_recv, id_send, id_recv, send_sem, r_sem, l_sem):
     tok = q_ref.shape[0]
@@ -30,6 +30,8 @@
     load_q = pltpu.make_async_copy(q_hbm, q_ref, load_sem.at[0])
     load_kv = pltpu.make_async_copy(kv_hbm, kv_buf.at[reach], load_sem.at[1])
     load_w = pltpu.make_async_copy(w_hbm, w_ref, load_sem.at[2])
+    load_ids = pltpu.make_async_copy(ids_hbm, id_buf.at[reach], load_sem.at[3])
+    load_ids.start()
     load_kv.start()
     load_q.start()
     load_w.start()
@@ -44,7 +46,7 @@
                 src_ref=source, dst_ref=target.at[slot], send_sem=sends.at[d - 1],
                 recv_sem=arrivals.at[2 * d - 1], device_id=(i + 2 * d, z), device_id_type=MESH)
             for source, target, sends, arrivals in (
-                (ids_ref, id_buf, id_send, id_recv), (kv_hbm, kv_buf, kv_send, kv_recv))]
+                (ids_hbm, id_buf, id_send, id_recv), (kv_hbm, kv_buf, kv_send, kv_recv))]
 
     def up_copies(d):
         return [
@@ -53,7 +55,7 @@
                 send_sem=sends.at[hops + d], recv_sem=arrivals.at[2 * d],
                 device_id=(i + 1, z), device_id_type=MESH)
             for source, target, sends, arrivals in (
-                (ids_ref, id_buf, id_send, id_recv), (kv_hbm, kv_buf, kv_send, kv_recv))]
+                (ids_hbm, id_buf, id_send, id_recv), (kv_hbm, kv_buf, kv_send, kv_recv))]
 
     def down_copies(d):
         return [
@@ -115,8 +117,8 @@
         def _():
             kv_buf[reach - k] = jnp.zeros(kv_buf.shape[1:], kv_buf.dtype)
             id_buf[reach - k] = jnp.full(id_buf.shape[1:], -1, id_buf.dtype)
-    id_buf[reach] = ids_ref[...]
-    own_ids = ids_ref[...].astype(jnp.float32)
+    load_ids.wait()
+    own_ids = id_buf[reach].astype(jnp.float32)
     square = (tok, tok)
     q_col[...] = jnp.max(
         jnp.where(lax.broadcasted_iota(jnp.int32, square, 0) == lax.broadcasted_iota(jnp.int32, square, 1),
@@ -233,13 +235,17 @@
         right_b = b - jnp.where(low_half, 1, 2)
         left_b = b - jnp.where(low_half, 2, 1)
 
-        @pl.when(middle & (right_b >= 0) & (right_b < blocks))
+        @pl.when(middle & low_half & (right_b >= 0) & (right_b < blocks))
         def _():
             forward_right(right_b)
 
         @pl.when(middle & (left_b >= 0) & (left_b < blocks))
         def _():
             forward_left(left_b)
+
+        @pl.when(middle & jnp.logical_not(low_half) & (right_b >= 0) & (right_b < blocks))
+        def _():
+            forward_right(right_b)
         return carry
 
     lax.fori_loop(0, blocks + 2, step, 0)
@@ -268,22 +274,22 @@
         @pl.when(z == 0)
         def _():
             left_copy(z, b).wait_recv()
-            out_ref[rows, :] = part[z, rows, :]
-            more_ref[rows, :] = recv_l[z, rows, :]
+            out_ref[rows, :] = (part[z, rows, :].astype(jnp.float32)
+                                + recv_l[z, rows, :].astype(jnp.float32)).astype(out_ref.dtype)
 
         @pl.when(z == n_tp - 1)
         def _():
             right_copy(z, b).wait_recv()
-            out_ref[rows, :] = part[z, rows, :]
-            more_ref[rows, :] = recv_r[z, rows, :]
+            out_ref[rows, :] = (part[z, rows, :].astype(jnp.float32)
+                                + recv_r[z, rows, :].astype(jnp.float32)).astype(out_ref.dtype)
 
         @pl.when(middle)
         def _():
             right_copy(z, b).wait_recv()
             left_copy(z, b).wait_recv()
-            out_ref[rows, :] = part[z, rows, :]
-            more_ref[rows, :] = (recv_r[z, rows, :].astype(jnp.float32)
-                                 + recv_l[z, rows, :].astype(jnp.float32)).astype(out_ref.dtype)
+            out_ref[rows, :] = (part[z, rows, :].astype(jnp.float32)
+                                + recv_r[z, rows, :].astype(jnp.float32)
+                                + recv_l[z, rows, :].astype(jnp.float32)).astype(out_ref.dtype)
         return carry
 
     lax.fori_loop(0, blocks, finish, 0)
@@ -337,11 +343,11 @@
     dma = pltpu.SemaphoreType.DMA
     any_spec = pl.BlockSpec(memory_space=pl.ANY)
     vmem_spec = pl.BlockSpec(memory_space=pltpu.VMEM)
-    one, more = pl.pallas_call(
+    return pl.pallas_call(
         functools.partial(kernel, n_loop, n_tp, reach),
-        out_shape=[jax.ShapeDtypeStruct((tok, width), jnp.bfloat16)] * 2,
-        in_specs=[any_spec, any_spec, vmem_spec, any_spec],
-        out_specs=[vmem_spec] * 2,
+        out_shape=pltpu.VMEM((tok, width), jnp.bfloat16),
+        in_specs=[any_spec] * 4,
+        out_specs=vmem_spec,
         scratch_shapes=[
             vmem((tok, q_cols), jnp.bfloat16),
             vmem((reach + 1, tok, 2 * HD), jnp.bfloat16),
@@ -354,14 +360,14 @@
             vmem((n_tp, tok, width), jnp.bfloat16),
             vmem((n_tp, tok, width), jnp.bfloat16),
             vmem((n_tp, tok, width), jnp.bfloat16),
-            dma((3,)), dma((reach,)), dma((reach,)), dma((reach,)), dma((reach,)),
+            dma((4,)), dma((reach,)), dma((reach,)), dma((reach,)), dma((reach,)),
             dma((n_tp, blocks)), dma((n_tp, blocks)), dma((n_tp, blocks)),
         ],
         compiler_params=pltpu.CompilerParams(
-            collective_id=0, has_side_effects=True, vmem_limit_bytes=56 * 1024 * 1024),
+            collective_id=0, has_side_effects=True, vmem_limit_bytes=32 * 1024 * 1024),
         cost_estimate=pl.CostEstimate(flops=3_500_000_000, bytes_accessed=10_000_000, transcendentals=2_000_000),
-    )(queries, key_values, prompt_ids.reshape(1, tok), out_weight)
-    return (one.astype(jnp.float32) + more.astype(jnp.float32)).astype(jnp.bfloat16)
+    )(*(pltpu.with_memory_space_constraint(x, pltpu.HBM)
+        for x in (queries, key_values, prompt_ids.reshape(1, tok), out_weight)))
 
 
 def solution(mesh):

time: 51.1 us -> 48.3 us (0.945)
  the two profiles are of different devices: /device:TPU:20 before, /device:TPU:21 now
where the time goes in v3:
time: 48.3 us; the launch traced here: 47.6 us
  Pallas kernels  46.8 us (97%)
  local copies, waits for them, and re-layouts  0.8 us (2%)
    pallas_call x1, Pallas kernels, per_device(): pl.pallas_call(functools.partial(kernel, n_loop, n_tp, reach), out_shape=...  46.8 us

profile of v3, /device:TPU:21, one launch (start us, length us, event | category | flops | bytes accessed | tf_op | source)
XLA Modules:
  0.0 47.6 jit_solution(18248870633063680515)
XLA Ops:
  0.0 46.8 %shard_map.46 = bf16[256,1024]{1,0:T(8,128)(2,1)S(1)} custom-call(bf16[256,1024]{1,0:T(8,128)(2,1)} %q_hbm.1, bf16[256,256]{1,0:T(8,128)(2,1)} %kv_hbm.1, s32[1,256]{1,0:T(1,128)} %bitcast.1, bf16[1024,4096]{1,0:T(8,128)(2,1)} %w_hbm.1), custom_call_target="tpu_custom_call" | custom-call | flops 3500000000 | bytes 10000000 | tf_op jit(solution)/shard_map/pallas_call | solution.py:346
  46.8 0.8 %copy.6 = bf16[256,1024]{1,0:T(8,128)(2,1)} copy(bf16[256,1024]{1,0:T(8,128)(2,1)S(1)} %shard_map.46) | data formatting | bytes 1048576

commit v4 on v3

--- a/solution.py
+++ b/solution.py
@@ -16,8 +16,8 @@
 
 
 def kernel(n_loop, n_tp, reach, q_hbm, kv_hbm, ids_hbm, w_hbm, out_ref,
-           q_ref, kv_buf, v_buf, id_buf, q_col, bias, attn, w_ref, part, recv_r, recv_l,
-           load_sem, kv_send, kv_recv, id_send, id_recv, send_sem, r_sem, l_sem):
+           q_ref, kv_buf, v_buf, id_buf, q_col, bias, probs, attn, w_ref, part, recv_r, recv_l,
+           load_sem, kv_send, kv_recv, relay_send, pair_send, pair_recv, id_send, id_recv, send_sem, r_sem, l_sem):
     tok = q_ref.shape[0]
     heads = q_ref.shape[1] // HD
     width = part.shape[2]
@@ -37,33 +37,96 @@
     load_w.start()
 
     core = lax.rem(i, 2)
+    chip = i // 2
     hops = reach // 2
 
-    def chip_copies(d):
-        slot = reach - 2 * d
-        return [
-            pltpu.make_async_remote_copy(
-                src_ref=source, dst_ref=target.at[slot], send_sem=sends.at[d - 1],
-                recv_sem=arrivals.at[2 * d - 1], device_id=(i + 2 * d, z), device_id_type=MESH)
-            for source, target, sends, arrivals in (
-                (ids_hbm, id_buf, id_send, id_recv), (kv_hbm, kv_buf, kv_send, kv_recv))]
-
-    def up_copies(d):
-        return [
-            pltpu.make_async_remote_copy(
-                src_ref=source if d == 0 else target.at[reach - 2 * d], dst_ref=target.at[reach - 2 * d - 1],
-                send_sem=sends.at[hops + d], recv_sem=arrivals.at[2 * d],
-                device_id=(i + 1, z), device_id_type=MESH)
-            for source, target, sends, arrivals in (
-                (ids_hbm, id_buf, id_send, id_recv), (kv_hbm, kv_buf, kv_send, kv_recv))]
-
-    def down_copies(d):
-        return [
-            pltpu.make_async_remote_copy(
-                src_ref=target.at[reach - 2 * d], dst_ref=target.at[reach - 2 * d + 1],
-                send_sem=sends.at[hops + d - 1], recv_sem=arrivals.at[2 * d - 2],
-                device_id=(i - 1, z), device_id_type=MESH)
-            for target, sends, arrivals in ((id_buf, id_send, id_recv), (kv_buf, kv_send, kv_recv))]
+    half = tok // 2
+    relay = n_loop == 8 and hops == 2
+
+    def id_chip(d):
+        return pltpu.make_async_remote_copy(
+            src_ref=ids_hbm, dst_ref=id_buf.at[reach - 2 * d], send_sem=id_send.at[d - 1],
+            recv_sem=id_recv.at[2 * d - 1], device_id=(i + 2 * d, z), device_id_type=MESH)
+
+    def id_up(d):
+        return pltpu.make_async_remote_copy(
+            src_ref=ids_hbm if d == 0 else id_buf.at[reach - 2 * d], dst_ref=id_buf.at[reach - 2 * d - 1],
+            send_sem=id_send.at[hops + d], recv_sem=id_recv.at[2 * d],
+            device_id=(i + 1, z), device_id_type=MESH)
+
+    def id_down(d):
+        return pltpu.make_async_remote_copy(
+            src_ref=id_buf.at[reach - 2 * d], dst_ref=id_buf.at[reach - 2 * d + 1],
+            send_sem=id_send.at[hops + d - 1], recv_sem=id_recv.at[2 * d - 2],
+            device_id=(i - 1, z), device_id_type=MESH)
+
+    def chip_copy(t, h, d):
+        rows, cols = pl.ds(h * half, half), pl.ds(t * HD, HD)
+        return pltpu.make_async_remote_copy(
+            src_ref=kv_hbm.at[rows, cols], dst_ref=kv_buf.at[reach - 2 * d, rows, cols],
+            send_sem=kv_send.at[t, h, d - 1], recv_sem=kv_recv.at[t, h, d - 1],
+            device_id=(i + 2 * d, z), device_id_type=MESH)
+
+    def relay_copy(t):
+        rows, cols = pl.ds(0, half), pl.ds(t * HD, HD)
+        return pltpu.make_async_remote_copy(
+            src_ref=kv_buf.at[reach - 4, rows, cols], dst_ref=kv_buf.at[reach - 2, rows, cols],
+            send_sem=relay_send.at[t], recv_sem=kv_recv.at[t, 0, 0],
+            device_id=(i - 2, z), device_id_type=MESH)
+
+    def up_copy(t, d):
+        cols = pl.ds(t * HD, HD)
+        return pltpu.make_async_remote_copy(
+            src_ref=kv_hbm.at[:, cols] if d == 0 else kv_buf.at[reach - 2 * d, :, cols],
+            dst_ref=kv_buf.at[reach - 2 * d - 1, :, cols],
+            send_sem=pair_send.at[t, d], recv_sem=pair_recv.at[t, d],
+            device_id=(i + 1, z), device_id_type=MESH)
+
+    def down_copy(t, d):
+        cols = pl.ds(t * HD, HD)
+        return pltpu.make_async_remote_copy(
+            src_ref=kv_buf.at[reach - 2 * d, :, cols], dst_ref=kv_buf.at[reach - 2 * d + 1, :, cols],
+            send_sem=pair_send.at[t, d - 1], recv_sem=pair_recv.at[t, d - 1],
+            device_id=(i - 1, z), device_id_type=MESH)
+
+    def chip_each(t, act):
+        for h in range(2):
+            for d in range(hops, 0, -1):
+                there = i + 2 * d < n_loop
+                if relay and h == 0 and d == 1:
+                    there = there & (chip != 1)
+
+                @pl.when(there)
+                def _():
+                    act(chip_copy(t, h, d))
+
+    def collect(t):
+        for d in range(hops, 0, -1):
+            @pl.when(i >= 2 * d)
+            def _():
+                chip_copy(t, 0, d).wait_recv()
+                if relay and d == 2:
+                    @pl.when(chip == 3)
+                    def _():
+                        relay_copy(t).start()
+                chip_copy(t, 1, d).wait_recv()
+
+                @pl.when(core == 1)
+                def _():
+                    down_copy(t, d).start()
+
+                if d < hops:
+                    @pl.when(core == 0)
+                    def _():
+                        up_copy(t, d).start()
+        for d in range(1, hops + 1):
+            @pl.when((core == 0) & (i >= 2 * d))
+            def _():
+                down_copy(t, d).wait_recv()
+
+            @pl.when((core == 1) & (i >= 2 * d - 1))
+            def _():
+                up_copy(t, d - 1).wait_recv()
 
     def right_copy(c, b):
         rows = pl.ds(pl.multiple_of(b * ROWS, ROWS), ROWS)
@@ -96,7 +159,6 @@
     def _():
         pl.semaphore_signal(barrier, inc=1, device_id=(i, z + 1), device_id_type=MESH)
 
-    chip = i // 2
     greeted = (1 + jnp.minimum(chip, hops) + jnp.minimum(n_loop // 2 - 1 - chip, hops)
                + jnp.minimum(z, 1) + jnp.minimum(n_tp - 1 - z, 1))
     pl.semaphore_wait(barrier, greeted)
@@ -104,13 +166,14 @@
     for d in range(1, hops + 1):
         @pl.when(i + 2 * d < n_loop)
         def _():
-            for copy in chip_copies(d):
-                copy.start()
+            id_chip(d).start()
+
+    chip_each(0, lambda copy: copy.start())
 
     @pl.when(core == 0)
     def _():
-        for copy in up_copies(0):
-            copy.start()
+        id_up(0).start()
+        up_copy(0, 0).start()
 
     for k in range(1, reach + 1):
         @pl.when(i < k)
@@ -126,34 +189,36 @@
     v_buf[:, HD:] = jnp.ones((v_buf.shape[0], HD), v_buf.dtype)
     load_kv.wait()
     load_q.wait()
+
+    chip_each(0, lambda copy: copy.wait_send())
+    chip_each(1, lambda copy: copy.start())
+
+    @pl.when(core == 0)
+    def _():
+        up_copy(1, 0).start()
+
     for d in range(1, hops + 1):
         @pl.when(i >= 2 * d)
         def _():
-            for copy in chip_copies(d):
-                copy.wait_recv()
+            id_chip(d).wait_recv()
 
             @pl.when(core == 1)
             def _():
-                for copy in down_copies(d):
-                    copy.start()
+                id_down(d).start()
 
             if d < hops:
                 @pl.when(core == 0)
                 def _():
-                    for copy in up_copies(d):
-                        copy.start()
+                    id_up(d).start()
+    collect(0)
     for d in range(1, hops + 1):
         @pl.when((core == 0) & (i >= 2 * d))
         def _():
-            for copy in down_copies(d):
-                copy.wait_recv()
+            id_down(d).wait_recv()
 
         @pl.when((core == 1) & (i >= 2 * d - 1))
         def _():
-            for copy in up_copies(d - 1):
-                copy.wait_recv()
-    for s in range(reach + 1):
-        v_buf[s * tok:(s + 1) * tok, :HD] = kv_buf[s, :, HD:]
+            id_up(d - 1).wait_recv()
 
     def compute(b):
         rows = pl.ds(pl.multiple_of(b * ROWS, ROWS), ROWS)
@@ -177,11 +242,18 @@
             first = p[:, :, :tok]
             p = jnp.concatenate(
                 [jnp.where(lower[None], 0.0, first), p[:, :, tok:], jnp.where(lower[None], first, 0.0)], axis=2)
-            p = p.reshape(STACK * ROWS, (reach + 1) * tok).astype(jnp.bfloat16)
-            o = jnp.dot(p, v_buf[...], preferred_element_type=jnp.float32)
-            o = (o[:, :HD] / o[:, HD:]).astype(jnp.bfloat16)
-            for j in range(STACK):
-                attn[:, (h + j) * HD:(h + j + 1) * HD] = o[j * ROWS:(j + 1) * ROWS]
+            probs[h * ROWS:(h + STACK) * ROWS, :] = p.reshape(STACK * ROWS, (reach + 1) * tok).astype(jnp.bfloat16)
+
+        @pl.when(b == 0)
+        def _():
+            collect(1)
+            for s in range(reach + 1):
+                v_buf[s * tok:(s + 1) * tok, :HD] = kv_buf[s, :, HD:]
+
+        o = jnp.dot(probs[...], v_buf[...], preferred_element_type=jnp.float32)
+        o = (o[:, :HD] / o[:, HD:]).astype(jnp.bfloat16)
+        for h in range(heads):
+            attn[:, h * HD:(h + 1) * HD] = o[h * ROWS:(h + 1) * ROWS]
 
         @pl.when(b == 0)
         def _():
@@ -294,21 +366,28 @@
 
     lax.fori_loop(0, blocks, finish, 0)
 
+    chip_each(1, lambda copy: copy.wait_send())
     for d in range(1, hops + 1):
         @pl.when(i + 2 * d < n_loop)
         def _():
-            for copy in chip_copies(d):
-                copy.wait_send()
+            id_chip(d).wait_send()
 
         @pl.when((core == 1) & (i >= 2 * d))
         def _():
-            for copy in down_copies(d):
-                copy.wait_send()
+            id_down(d).wait_send()
+            for t in range(2):
+                down_copy(t, d).wait_send()
 
         @pl.when((core == 0) & (i >= 2 * d - 2))
         def _():
-            for copy in up_copies(d - 1):
-                copy.wait_send()
+            id_up(d - 1).wait_send()
+            for t in range(2):
+                up_copy(t, d - 1).wait_send()
+    if relay:
+        @pl.when(chip == 3)
+        def _():
+            for t in range(2):
+                relay_copy(t).wait_send()
 
     def drain(b, carry):
         @pl.when(z == 0)
@@ -339,6 +418,7 @@
     width = d_out // n_tp
     reach = min(8, n_loop // 2)
     blocks = tok // ROWS
+    hops = reach // 2
     vmem = pltpu.VMEM
     dma = pltpu.SemaphoreType.DMA
     any_spec = pl.BlockSpec(memory_space=pl.ANY)
@@ -355,12 +435,14 @@
             vmem((reach + 1, 1, tok), jnp.int32),
             vmem((tok, 1), jnp.float32),
             vmem((ROWS, reach * tok), jnp.float32),
+            vmem((q_cols // HD * ROWS, (reach + 1) * tok), jnp.bfloat16),
             vmem((ROWS, q_cols), jnp.bfloat16),
             vmem((depth, d_out), jnp.bfloat16),
             vmem((n_tp, tok, width), jnp.bfloat16),
             vmem((n_tp, tok, width), jnp.bfloat16),
             vmem((n_tp, tok, width), jnp.bfloat16),
-            dma((4,)), dma((reach,)), dma((reach,)), dma((reach,)), dma((reach,)),
+            dma((4,)), dma((2, 2, hops)), dma((2, 2, hops)), dma((2,)), dma((2, hops)), dma((2, hops)),
+            dma((reach,)), dma((reach,)),
             dma((n_tp, blocks)), dma((n_tp, blocks)), dma((n_tp, blocks)),
         ],
         compiler_params=pltpu.CompilerParams(

time: 48.3 us -> 52.1 us (1.079); the launches traced: 47.6 us -> 52 us
  Pallas kernels: 46.8 us -> 51.2 us
    pallas_call x1, Pallas kernels: 46.8 us -> 51.2 us  [per_device(): pl.pallas_call(functools.partial(kernel, n_loop, n_tp, reach), out_shape=...]
where the time goes in v4:
time: 52.1 us; the launch traced here: 52 us
  Pallas kernels  51.2 us (98%)
  local copies, waits for them, and re-layouts  0.8 us (2%)
    pallas_call x1, Pallas kernels, per_device(): pl.pallas_call(functools.partial(kernel, n_loop, n_tp, reach), out_shape=...  51.2 us

profile of v4, /device:TPU:21, one launch (start us, length us, event | category | flops | bytes accessed | tf_op | source)
XLA Modules:
  0.0 52.0 jit_solution(17793700107051774069)
XLA Ops:
  0.0 51.2 %shard_map.46 = bf16[256,1024]{1,0:T(8,128)(2,1)S(1)} custom-call(bf16[256,1024]{1,0:T(8,128)(2,1)} %q_hbm.1, bf16[256,256]{1,0:T(8,128)(2,1)} %kv_hbm.1, s32[1,256]{1,0:T(1,128)} %bitcast.1, bf16[1024,4096]{1,0:T(8,128)(2,1)} %w_hbm.1), custom_call_target="tpu_custom_call" | custom-call | flops 3500000000 | bytes 10000000 | tf_op jit(solution)/shard_map/pallas_call | solution.py:426
  51.2 0.8 %copy.6 = bf16[256,1024]{1,0:T(8,128)(2,1)} copy(bf16[256,1024]{1,0:T(8,128)(2,1)S(1)} %shard_map.46) | data formatting | bytes 1048576

commit v5 on v3

--- a/solution.py
+++ b/solution.py
@@ -16,7 +16,7 @@
 
 
 def kernel(n_loop, n_tp, reach, q_hbm, kv_hbm, ids_hbm, w_hbm, out_ref,
-           q_ref, kv_buf, v_buf, id_buf, q_col, bias, attn, w_ref, part, recv_r, recv_l,
+           q_ref, kv_buf, k_t, v_buf, id_buf, q_col, bias, attn, w_ref, part, recv_r, recv_l,
            load_sem, kv_send, kv_recv, id_send, id_recv, send_sem, r_sem, l_sem):
     tok = q_ref.shape[0]
     heads = q_ref.shape[1] // HD
@@ -153,7 +153,10 @@
             for copy in up_copies(d - 1):
                 copy.wait_recv()
     for s in range(reach + 1):
+        k_t[:, s * tok:(s + 1) * tok] = kv_buf[s, :, :HD].T
         v_buf[s * tok:(s + 1) * tok, :HD] = kv_buf[s, :, HD:]
+
+    low_half = z < n_tp // 2
 
     def compute(b):
         rows = pl.ds(pl.multiple_of(b * ROWS, ROWS), ROWS)
@@ -165,10 +168,9 @@
         shared = jnp.where(lower, key_ids[reach], key_ids[0])
         for s, ids in enumerate([shared] + key_ids[1:reach]):
             bias[:, s * tok:(s + 1) * tok] = jnp.where(ids == q_ids, 0.0, BLOCKED)
-        keys = kv_buf[:, :, :HD].reshape((reach + 1) * tok, HD)
         for h in range(0, heads, STACK):
             q = jnp.concatenate([q_ref[rows, (h + j) * HD:(h + j + 1) * HD] for j in range(STACK)], axis=0)
-            s = lax.dot_general(q, keys, (((1,), (1,)), ((), ())), preferred_element_type=jnp.float32)
+            s = jnp.dot(q, k_t[...], preferred_element_type=jnp.float32)
             s = s.reshape(STACK, ROWS, (reach + 1) * tok)
             s = jnp.concatenate(
                 [jnp.where(lower[None], s[:, :, far_last:], s[:, :, :tok]), s[:, :, tok:far_last]], axis=2)
@@ -181,26 +183,34 @@
             o = jnp.dot(p, v_buf[...], preferred_element_type=jnp.float32)
             o = (o[:, :HD] / o[:, HD:]).astype(jnp.bfloat16)
             for j in range(STACK):
-                attn[:, (h + j) * HD:(h + j + 1) * HD] = o[j * ROWS:(j + 1) * ROWS]
+                attn[rows, (h + j) * HD:(h + j + 1) * HD] = o[j * ROWS:(j + 1) * ROWS]
 
         @pl.when(b == 0)
         def _():
             load_w.wait()
-        order = []
-        for c in range((n_tp + 1) // 2):
-            order += [n_tp - 1 - c, c] if c != n_tp - 1 - c else [c]
-        for c in order:
+
+    def project(b, count):
+        rows = pl.ds(pl.multiple_of(b * ROWS, ROWS), count * ROWS)
+        heads_out = attn[rows, :]
+
+        def one(j, carry):
+            c = jnp.where(low_half, n_tp - 1 - j, j)
             part[c, rows, :] = jnp.dot(
-                attn[...], w_ref[:, c * width:(c + 1) * width],
+                heads_out, w_ref[:, pl.ds(pl.multiple_of(c * width, width), width)],
                 preferred_element_type=jnp.float32).astype(jnp.bfloat16)
-            if c >= 2:
-                @pl.when(z == 0)
-                def _():
-                    right_copy(c, b).start()
-            if c < n_tp - 2:
-                @pl.when(z == n_tp - 1)
-                def _():
-                    left_copy(c, b).start()
+
+            @pl.when((z == 0) & (c >= 2))
+            def _():
+                for n in range(count):
+                    right_copy(c, b + n).start()
+
+            @pl.when((z == n_tp - 1) & (c < n_tp - 2))
+            def _():
+                for n in range(count):
+                    left_copy(c, b + n).start()
+            return carry
+
+        lax.fori_loop(0, n_tp, one, 0)
 
     def forward_right(b):
         rows = pl.ds(pl.multiple_of(b * ROWS, ROWS), ROWS)
@@ -224,13 +234,30 @@
                                     + recv_l[c, rows, :].astype(jnp.float32)).astype(jnp.bfloat16)
                 copy.start()
 
-    low_half = z < n_tp // 2
     middle = jnp.logical_and(z > 0, z < n_tp - 1)
 
     def step(b, carry):
         @pl.when(b < blocks)
         def _():
             compute(b)
+
+        @pl.when(b < 2)
+        def _():
+            project(b, 1)
+
+        @pl.when((b < blocks) & (b > 2) & (b % 2 == 1))
+        def _():
+            project(b - 1, 2)
+
+        late = b - blocks // 2
+
+        @pl.when((z == 0) & (late >= 0) & (b < blocks))
+        def _():
+            right_copy(1, late).start()
+
+        @pl.when((z == n_tp - 1) & (late >= 0) & (b < blocks))
+        def _():
+            left_copy(n_tp - 2, late).start()
 
         right_b = b - jnp.where(low_half, 1, 2)
         left_b = b - jnp.where(low_half, 2, 1)
@@ -256,7 +283,7 @@
             for c in range(n_tp - 1, 1, -1):
                 right_copy(c, b).wait_send()
             if b == blocks - 2:
-                for late in range(blocks):
+                for late in range(blocks // 2, blocks):
                     right_copy(1, late).start()
 
     @pl.when(z == n_tp - 1)
@@ -265,7 +292,7 @@
             for c in range(n_tp - 2):
                 left_copy(c, b).wait_send()
             if b == blocks - 2:
-                for late in range(blocks):
+                for late in range(blocks // 2, blocks):
                     left_copy(n_tp - 2, late).start()
 
     def finish(b, carry):
@@ -351,11 +378,12 @@
         scratch_shapes=[
             vmem((tok, q_cols), jnp.bfloat16),
             vmem((reach + 1, tok, 2 * HD), jnp.bfloat16),
+            vmem((HD, (reach + 1) * tok), jnp.bfloat16),
             vmem(((reach + 1) * tok, 2 * HD), jnp.bfloat16),
             vmem((reach + 1, 1, tok), jnp.int32),
             vmem((tok, 1), jnp.float32),
             vmem((ROWS, reach * tok), jnp.float32),
-            vmem((ROWS, q_cols), jnp.bfloat16),
+            vmem((tok, q_cols), jnp.bfloat16),
             vmem((depth, d_out), jnp.bfloat16),
             vmem((n_tp, tok, width), jnp.bfloat16),
             vmem((n_tp, tok, width), jnp.bfloat16),

time: 48.3 us -> 50.5 us (1.046)
  the two profiles are of different devices: /device:TPU:21 before, /device:TPU:4 now
where the time goes in v5:
time: 50.5 us; the launch traced here: 50.3 us
  Pallas kernels  49.5 us (98%)
  local copies, waits for them, and re-layouts  0.8 us (2%)
    pallas_call x1, Pallas kernels, per_device(): pl.pallas_call(functools.partial(kernel, n_loop, n_tp, reach), out_shape=...  49.5 us

profile of v5, /device:TPU:4, one launch (start us, length us, event | category | flops | bytes accessed | tf_op | source)
XLA Modules:
  0.0 50.3 jit_solution(11479055595741630291)
XLA Ops:
  0.0 49.5 %shard_map.46 = bf16[256,1024]{1,0:T(8,128)(2,1)S(1)} custom-call(bf16[256,1024]{1,0:T(8,128)(2,1)} %q_hbm.1, bf16[256,256]{1,0:T(8,128)(2,1)} %kv_hbm.1, s32[1,256]{1,0:T(1,128)} %bitcast.1, bf16[1024,4096]{1,0:T(8,128)(2,1)} %w_hbm.1), custom_call_target="tpu_custom_call" | custom-call | flops 3500000000 | bytes 10000000 | tf_op jit(solution)/shard_map/pallas_call | solution.py:373
  49.5 0.8 %copy.6 = bf16[256,1024]{1,0:T(8,128)(2,1)} copy(bf16[256,1024]{1,0:T(8,128)(2,1)S(1)} %shard_map.46) | data formatting | bytes 1048576

commit v6 on v3

--- a/solution.py
+++ b/solution.py
@@ -17,7 +17,7 @@
 
 def kernel(n_loop, n_tp, reach, q_hbm, kv_hbm, ids_hbm, w_hbm, out_ref,
            q_ref, kv_buf, v_buf, id_buf, q_col, bias, attn, w_ref, part, recv_r, recv_l,
-           load_sem, kv_send, kv_recv, id_send, id_recv, send_sem, r_sem, l_sem):
+           load_sem, w_sem, kv_send, kv_recv, chip_send, chip_recv, relay_send, id_send, id_recv, send_sem, r_sem, l_sem):
     tok = q_ref.shape[0]
     heads = q_ref.shape[1] // HD
     width = part.shape[2]
@@ -29,24 +29,56 @@
 
     load_q = pltpu.make_async_copy(q_hbm, q_ref, load_sem.at[0])
     load_kv = pltpu.make_async_copy(kv_hbm, kv_buf.at[reach], load_sem.at[1])
-    load_w = pltpu.make_async_copy(w_hbm, w_ref, load_sem.at[2])
-    load_ids = pltpu.make_async_copy(ids_hbm, id_buf.at[reach], load_sem.at[3])
+    low_half = z < n_tp // 2
+
+    def load_w(j):
+        c = jnp.where(low_half, n_tp - 1 - j, j)
+        cols = pl.ds(pl.multiple_of(c * width, width), width)
+        return pltpu.make_async_copy(w_hbm.at[:, cols], w_ref.at[:, cols], w_sem.at[j])
+
+    load_ids = pltpu.make_async_copy(ids_hbm, id_buf.at[reach], load_sem.at[2])
     load_ids.start()
     load_kv.start()
     load_q.start()
-    load_w.start()
+    for j in range(n_tp):
+        load_w(j).start()
 
     core = lax.rem(i, 2)
+    chip = i // 2
     hops = reach // 2
 
-    def chip_copies(d):
-        slot = reach - 2 * d
-        return [
-            pltpu.make_async_remote_copy(
-                src_ref=source, dst_ref=target.at[slot], send_sem=sends.at[d - 1],
-                recv_sem=arrivals.at[2 * d - 1], device_id=(i + 2 * d, z), device_id_type=MESH)
-            for source, target, sends, arrivals in (
-                (ids_hbm, id_buf, id_send, id_recv), (kv_hbm, kv_buf, kv_send, kv_recv))]
+    half = tok // 2
+    relay = n_loop == 8 and hops == 2
+
+    def id_chip(d):
+        return pltpu.make_async_remote_copy(
+            src_ref=ids_hbm, dst_ref=id_buf.at[reach - 2 * d], send_sem=id_send.at[d - 1],
+            recv_sem=id_recv.at[2 * d - 1], device_id=(i + 2 * d, z), device_id_type=MESH)
+
+    def kv_chip(h, d):
+        rows = pl.ds(h * half, half)
+        return pltpu.make_async_remote_copy(
+            src_ref=kv_hbm.at[rows], dst_ref=kv_buf.at[reach - 2 * d, rows],
+            send_sem=chip_send.at[h, d - 1], recv_sem=chip_recv.at[h, d - 1],
+            device_id=(i + 2 * d, z), device_id_type=MESH)
+
+    def kv_relay():
+        rows = pl.ds(0, half)
+        return pltpu.make_async_remote_copy(
+            src_ref=kv_buf.at[reach - 4, rows], dst_ref=kv_buf.at[reach - 2, rows],
+            send_sem=relay_send.at[0], recv_sem=chip_recv.at[0, 0],
+            device_id=(i - 2, z), device_id_type=MESH)
+
+    def chip_each(act):
+        for h in range(2):
+            for d in range(hops, 0, -1):
+                there = i + 2 * d < n_loop
+                if relay and h == 0 and d == 1:
+                    there = there & (chip != 1)
+
+                @pl.when(there)
+                def _():
+                    act(kv_chip(h, d))
 
     def up_copies(d):
         return [
@@ -96,7 +128,6 @@
     def _():
         pl.semaphore_signal(barrier, inc=1, device_id=(i, z + 1), device_id_type=MESH)
 
-    chip = i // 2
     greeted = (1 + jnp.minimum(chip, hops) + jnp.minimum(n_loop // 2 - 1 - chip, hops)
                + jnp.minimum(z, 1) + jnp.minimum(n_tp - 1 - z, 1))
     pl.semaphore_wait(barrier, greeted)
@@ -104,8 +135,9 @@
     for d in range(1, hops + 1):
         @pl.when(i + 2 * d < n_loop)
         def _():
-            for copy in chip_copies(d):
-                copy.start()
+            id_chip(d).start()
+
+    chip_each(lambda copy: copy.start())
 
     @pl.when(core == 0)
     def _():
@@ -126,11 +158,16 @@
     v_buf[:, HD:] = jnp.ones((v_buf.shape[0], HD), v_buf.dtype)
     load_kv.wait()
     load_q.wait()
-    for d in range(1, hops + 1):
+    for d in range(hops, 0, -1):
         @pl.when(i >= 2 * d)
         def _():
-            for copy in chip_copies(d):
-                copy.wait_recv()
+            id_chip(d).wait_recv()
+            kv_chip(0, d).wait_recv()
+            if relay and d == 2:
+                @pl.when(chip == 3)
+                def _():
+                    kv_relay().start()
+            kv_chip(1, d).wait_recv()
 
             @pl.when(core == 1)
             def _():
@@ -183,24 +220,24 @@
             for j in range(STACK):
                 attn[:, (h + j) * HD:(h + j + 1) * HD] = o[j * ROWS:(j + 1) * ROWS]
 
-        @pl.when(b == 0)
-        def _():
-            load_w.wait()
-        order = []
-        for c in range((n_tp + 1) // 2):
-            order += [n_tp - 1 - c, c] if c != n_tp - 1 - c else [c]
-        for c in order:
+        for j in range(n_tp):
+            c = jnp.where(low_half, n_tp - 1 - j, j)
+
+            @pl.when(b == 0)
+            def _():
+                load_w(j).wait()
+
             part[c, rows, :] = jnp.dot(
-                attn[...], w_ref[:, c * width:(c + 1) * width],
+                attn[...], w_ref[:, pl.ds(pl.multiple_of(c * width, width), width)],
                 preferred_element_type=jnp.float32).astype(jnp.bfloat16)
-            if c >= 2:
-                @pl.when(z == 0)
-                def _():
-                    right_copy(c, b).start()
-            if c < n_tp - 2:
-                @pl.when(z == n_tp - 1)
-                def _():
-                    left_copy(c, b).start()
+
+            @pl.when((z == 0) & (c >= 2))
+            def _():
+                right_copy(c, b).start()
+
+            @pl.when((z == n_tp - 1) & (c < n_tp - 2))
+            def _():
+                left_copy(c, b).start()
 
     def forward_right(b):
         rows = pl.ds(pl.multiple_of(b * ROWS, ROWS), ROWS)
@@ -224,7 +261,6 @@
                                     + recv_l[c, rows, :].astype(jnp.float32)).astype(jnp.bfloat16)
                 copy.start()
 
-    low_half = z < n_tp // 2
     middle = jnp.logical_and(z > 0, z < n_tp - 1)
 
     def step(b, carry):
@@ -294,11 +330,15 @@
 
     lax.fori_loop(0, blocks, finish, 0)
 
+    chip_each(lambda copy: copy.wait_send())
+    if relay:
+        @pl.when(chip == 3)
+        def _():
+            kv_relay().wait_send()
     for d in range(1, hops + 1):
         @pl.when(i + 2 * d < n_loop)
         def _():
-            for copy in chip_copies(d):
-                copy.wait_send()
+            id_chip(d).wait_send()
 
         @pl.when((core == 1) & (i >= 2 * d))
         def _():
@@ -339,6 +379,7 @@
     width = d_out // n_tp
     reach = min(8, n_loop // 2)
     blocks = tok // ROWS
+    hops = reach // 2
     vmem = pltpu.VMEM
     dma = pltpu.SemaphoreType.DMA
     any_spec = pl.BlockSpec(memory_space=pl.ANY)
@@ -360,7 +401,8 @@
             vmem((n_tp, tok, width), jnp.bfloat16),
             vmem((n_tp, tok, width), jnp.bfloat16),
             vmem((n_tp, tok, width), jnp.bfloat16),
-            dma((4,)), dma((reach,)), dma((reach,)), dma((reach,)), dma((reach,)),
+            dma((3,)), dma((n_tp,)), dma((reach,)), dma((reach,)), dma((2, hops)), dma((2, hops)), dma((1,)),
+            dma((reach,)), dma((reach,)),
             dma((n_tp, blocks)), dma((n_tp, blocks)), dma((n_tp, blocks)),
         ],
         compiler_params=pltpu.CompilerParams(

time: 48.3 us -> 49.1 us (1.017); the launches traced: 47.6 us -> 49 us
  Pallas kernels: 46.8 us -> 48.2 us
    pallas_call x1, Pallas kernels: 46.8 us -> 48.2 us  [per_device(): pl.pallas_call(functools.partial(kernel, n_loop, n_tp, reach), out_shape=...]
where the time goes in v6:
time: 49.1 us; the launch traced here: 49 us
  Pallas kernels  48.2 us (98%)
  local copies, waits for them, and re-layouts  0.8 us (2%)
    pallas_call x1, Pallas kernels, per_device(): pl.pallas_call(functools.partial(kernel, n_loop, n_tp, reach), out_shape=...  48.2 us

profile of v6, /device:TPU:21, one launch (start us, length us, event | category | flops | bytes accessed | tf_op | source)
XLA Modules:
  0.0 49.0 jit_solution(2778021788565381062)
XLA Ops:
  0.0 48.2 %shard_map.46 = bf16[256,1024]{1,0:T(8,128)(2,1)S(1)} custom-call(bf16[256,1024]{1,0:T(8,128)(2,1)} %q_hbm.1, bf16[256,256]{1,0:T(8,128)(2,1)} %kv_hbm.1, s32[1,256]{1,0:T(1,128)} %bitcast.1, bf16[1024,4096]{1,0:T(8,128)(2,1)} %w_hbm.1), custom_call_target="tpu_custom_call" | custom-call | flops 3500000000 | bytes 10000000 | tf_op jit(solution)/shard_map/pallas_call | solution.py:387
  48.2 0.8 %copy.6 = bf16[256,1024]{1,0:T(8,128)(2,1)} copy(bf16[256,1024]{1,0:T(8,128)(2,1)S(1)} %shard_map.46) | data formatting | bytes 1048576

commit v7 on v6

--- a/solution.py
+++ b/solution.py
@@ -16,8 +16,8 @@
 
 
 def kernel(n_loop, n_tp, reach, q_hbm, kv_hbm, ids_hbm, w_hbm, out_ref,
-           q_ref, kv_buf, v_buf, id_buf, q_col, bias, attn, w_ref, part, recv_r, recv_l,
-           load_sem, w_sem, kv_send, kv_recv, chip_send, chip_recv, relay_send, id_send, id_recv, send_sem, r_sem, l_sem):
+           q_ref, kv_buf, v_buf, id_buf, q_col, bias, attn, w_ref, part, recv_r, recv_l, side_a, side_b,
+           load_sem, w_sem, kv_send, kv_recv, chip_send, chip_recv, side_sem, id_send, id_recv, send_sem, r_sem, l_sem):
     tok = q_ref.shape[0]
     heads = q_ref.shape[1] // HD
     width = part.shape[2]
@@ -48,7 +48,6 @@
     hops = reach // 2
 
     half = tok // 2
-    relay = n_loop == 8 and hops == 2
 
     def id_chip(d):
         return pltpu.make_async_remote_copy(
@@ -62,21 +61,10 @@
             send_sem=chip_send.at[h, d - 1], recv_sem=chip_recv.at[h, d - 1],
             device_id=(i + 2 * d, z), device_id_type=MESH)
 
-    def kv_relay():
-        rows = pl.ds(0, half)
-        return pltpu.make_async_remote_copy(
-            src_ref=kv_buf.at[reach - 4, rows], dst_ref=kv_buf.at[reach - 2, rows],
-            send_sem=relay_send.at[0], recv_sem=chip_recv.at[0, 0],
-            device_id=(i - 2, z), device_id_type=MESH)
-
     def chip_each(act):
         for h in range(2):
             for d in range(hops, 0, -1):
-                there = i + 2 * d < n_loop
-                if relay and h == 0 and d == 1:
-                    there = there & (chip != 1)
-
-                @pl.when(there)
+                @pl.when(i + 2 * d < n_loop)
                 def _():
                     act(kv_chip(h, d))
 
@@ -108,6 +96,24 @@
         return pltpu.make_async_remote_copy(
             src_ref=part.at[c, rows], dst_ref=recv_l.at[c, rows], send_sem=send_sem.at[c, b],
             recv_sem=l_sem.at[c, b], device_id=(i, z - 1), device_id_type=MESH)
+
+    side = n_loop == 8 and n_tp >= 4 and reach == 4
+    given = 2 if side else 0
+
+    def side_first(c, b):
+        return pltpu.make_async_remote_copy(
+            src_ref=part.at[c, pl.ds(b * ROWS, ROWS)], dst_ref=side_a.at[b], send_sem=side_sem.at[0, b],
+            recv_sem=side_sem.at[1, b], device_id=(i - 4, z), device_id_type=MESH)
+
+    def side_second(step, b):
+        return pltpu.make_async_remote_copy(
+            src_ref=side_a.at[b], dst_ref=side_b.at[b], send_sem=side_sem.at[2, b],
+            recv_sem=side_sem.at[3, b], device_id=(i, z + step), device_id_type=MESH)
+
+    def side_third(c, target, sems, b):
+        return pltpu.make_async_remote_copy(
+            src_ref=side_b.at[b], dst_ref=target.at[c, pl.ds(b * ROWS, ROWS)], send_sem=side_sem.at[4, b],
+            recv_sem=sems.at[c, b], device_id=(i + 4, z), device_id_type=MESH)
 
     barrier = pltpu.get_barrier_semaphore()
     pl.semaphore_signal(barrier, inc=1, device_id=(i + 1 - 2 * core, z), device_id_type=MESH)
@@ -163,10 +169,6 @@
         def _():
             id_chip(d).wait_recv()
             kv_chip(0, d).wait_recv()
-            if relay and d == 2:
-                @pl.when(chip == 3)
-                def _():
-                    kv_relay().start()
             kv_chip(1, d).wait_recv()
 
             @pl.when(core == 1)
@@ -239,6 +241,15 @@
             def _():
                 left_copy(c, b).start()
 
+        for n in range(given):
+            @pl.when((b == n) & (chip == 2) & (z == 0))
+            def _():
+                side_first(1, n).start()
+
+            @pl.when((b == n) & (chip == 2) & (z == n_tp - 1))
+            def _():
+                side_first(n_tp - 2, n).start()
+
     def forward_right(b):
         rows = pl.ds(pl.multiple_of(b * ROWS, ROWS), ROWS)
         for c in range(n_tp - 1, 1, -1):
@@ -285,6 +296,19 @@
         return carry
 
     lax.fori_loop(0, blocks + 2, step, 0)
+
+    def send_late(near, copy, step):
+        for n in range(given):
+            @pl.when(chip == 0)
+            def _():
+                side_first(near, n).wait_recv()
+                side_second(step, n).start()
+
+            @pl.when(chip != 2)
+            def _():
+                copy(near, n).start()
+        for late in range(given, blocks):
+            copy(near, late).start()
 
     @pl.when(z == 0)
     def _():
@@ -292,8 +316,7 @@
             for c in range(n_tp - 1, 1, -1):
                 right_copy(c, b).wait_send()
             if b == blocks - 2:
-                for late in range(blocks):
-                    right_copy(1, late).start()
+                send_late(1, right_copy, 1)
 
     @pl.when(z == n_tp - 1)
     def _():
@@ -301,10 +324,21 @@
             for c in range(n_tp - 2):
                 left_copy(c, b).wait_send()
             if b == blocks - 2:
-                for late in range(blocks):
-                    left_copy(n_tp - 2, late).start()
-
-    def finish(b, carry):
+                send_late(n_tp - 2, left_copy, -1)
+
+    for n in range(given):
+        @pl.when((chip == 0) & (z == 1))
+        def _():
+            side_second(1, n).wait_recv()
+            side_third(1, recv_r, r_sem, n).start()
+
+        @pl.when((chip == 0) & (z == n_tp - 2))
+        def _():
+            side_second(-1, n).wait_recv()
+            side_third(n_tp - 2, recv_l, l_sem, n).start()
+
+    def finish(n, carry):
+        b = lax.rem(n + given, blocks)
         rows = pl.ds(pl.multiple_of(b * ROWS, ROWS), ROWS)
 
         @pl.when(z == 0)
@@ -331,10 +365,6 @@
     lax.fori_loop(0, blocks, finish, 0)
 
     chip_each(lambda copy: copy.wait_send())
-    if relay:
-        @pl.when(chip == 3)
-        def _():
-            kv_relay().wait_send()
     for d in range(1, hops + 1):
         @pl.when(i + 2 * d < n_loop)
         def _():
@@ -350,12 +380,39 @@
             for copy in up_copies(d - 1):
                 copy.wait_send()
 
+    for n in range(given):
+        @pl.when((chip == 2) & (z == 0))
+        def _():
+            side_first(1, n).wait_send()
+
+        @pl.when((chip == 2) & (z == n_tp - 1))
+        def _():
+            side_first(n_tp - 2, n).wait_send()
+
+        @pl.when((chip == 0) & (z == 0))
+        def _():
+            side_second(1, n).wait_send()
+
+        @pl.when((chip == 0) & (z == n_tp - 1))
+        def _():
+            side_second(-1, n).wait_send()
+
+        @pl.when((chip == 0) & (z == 1))
+        def _():
+            side_third(1, recv_r, r_sem, n).wait_send()
+
+        @pl.when((chip == 0) & (z == n_tp - 2))
+        def _():
+            side_third(n_tp - 2, recv_l, l_sem, n).wait_send()
+
     def drain(b, carry):
-        @pl.when(z == 0)
+        direct = (b >= given) | (chip != 2)
+
+        @pl.when((z == 0) & direct)
         def _():
             right_copy(1, b).wait_send()
 
-        @pl.when(z == n_tp - 1)
+        @pl.when((z == n_tp - 1) & direct)
         def _():
             left_copy(n_tp - 2, b).wait_send()
 
@@ -401,7 +458,9 @@
             vmem((n_tp, tok, width), jnp.bfloat16),
             vmem((n_tp, tok, width), jnp.bfloat16),
             vmem((n_tp, tok, width), jnp.bfloat16),
-            dma((3,)), dma((n_tp,)), dma((reach,)), dma((reach,)), dma((2, hops)), dma((2, hops)), dma((1,)),
+            vmem((2, ROWS, width), jnp.bfloat16),
+            vmem((2, ROWS, width), jnp.bfloat16),
+            dma((3,)), dma((n_tp,)), dma((reach,)), dma((reach,)), dma((2, hops)), dma((2, hops)), dma((5, 2)),
             dma((reach,)), dma((reach,)),
             dma((n_tp, blocks)), dma((n_tp, blocks)), dma((n_tp, blocks)),
         ],

time: 49.1 us -> 47.1 us (0.959); the launches traced: 49 us -> 46.3 us
  Pallas kernels: 48.2 us -> 45.5 us
    pallas_call x1, Pallas kernels: 48.2 us -> 45.5 us  [per_device(): pl.pallas_call(functools.partial(kernel, n_loop, n_tp, reach), out_shape=...]
where the time goes in v7:
time: 47.1 us; the launch traced here: 46.3 us
  Pallas kernels  45.5 us (97%)
  local copies, waits for them, and re-layouts  0.8 us (2%)
    pallas_call x1, Pallas kernels, per_device(): pl.pallas_call(functools.partial(kernel, n_loop, n_tp, reach), out_shape=...  45.5 us

profile of v7, /device:TPU:21, one launch (start us, length us, event | category | flops | bytes accessed | tf_op | source)
XLA Modules:
  0.0 46.3 jit_solution(9886499479714445575)
XLA Ops:
  0.0 45.5 %shard_map.46 = bf16[256,1024]{1,0:T(8,128)(2,1)S(1)} custom-call(bf16[256,1024]{1,0:T(8,128)(2,1)} %q_hbm.1, bf16[256,256]{1,0:T(8,128)(2,1)} %kv_hbm.1, s32[1,256]{1,0:T(1,128)} %bitcast.1, bf16[1024,4096]{1,0:T(8,128)(2,1)} %w_hbm.1), custom_call_target="tpu_custom_call" | custom-call | flops 3500000000 | bytes 10000000 | tf_op jit(solution)/shard_map/pallas_call | solution.py:444
  45.6 0.8 %copy.6 = bf16[256,1024]{1,0:T(8,128)(2,1)} copy(bf16[256,1024]{1,0:T(8,128)(2,1)S(1)} %shard_map.46) | data formatting | bytes 1048576

commit v8 on v7

--- a/solution.py
+++ b/solution.py
@@ -37,11 +37,6 @@
         return pltpu.make_async_copy(w_hbm.at[:, cols], w_ref.at[:, cols], w_sem.at[j])
 
     load_ids = pltpu.make_async_copy(ids_hbm, id_buf.at[reach], load_sem.at[2])
-    load_ids.start()
-    load_kv.start()
-    load_q.start()
-    for j in range(n_tp):
-        load_w(j).start()
 
     core = lax.rem(i, 2)
     chip = i // 2
@@ -136,6 +131,11 @@
 
     greeted = (1 + jnp.minimum(chip, hops) + jnp.minimum(n_loop // 2 - 1 - chip, hops)
                + jnp.minimum(z, 1) + jnp.minimum(n_tp - 1 - z, 1))
+    load_ids.start()
+    load_kv.start()
+    load_q.start()
+    for j in range(n_tp):
+        load_w(j).start()
     pl.semaphore_wait(barrier, greeted)
 
     for d in range(1, hops + 1):
@@ -337,6 +337,44 @@
             side_second(-1, n).wait_recv()
             side_third(n_tp - 2, recv_l, l_sem, n).start()
 
+    chip_each(lambda copy: copy.wait_send())
+    for d in range(1, hops + 1):
+        @pl.when(i + 2 * d < n_loop)
+        def _():
+            id_chip(d).wait_send()
+
+        @pl.when((core == 1) & (i >= 2 * d))
+        def _():
+            for copy in down_copies(d):
+                copy.wait_send()
+
+        @pl.when((core == 0) & (i >= 2 * d - 2))
+        def _():
+            for copy in up_copies(d - 1):
+                copy.wait_send()
+
+    for n in range(given):
+        @pl.when((chip == 2) & (z == 0))
+        def _():
+            side_first(1, n).wait_send()
+
+        @pl.when((chip == 2) & (z == n_tp - 1))
+        def _():
+            side_first(n_tp - 2, n).wait_send()
+
+    def drain(b, carry):
+        for c in range(n_tp):
+            @pl.when(middle & (c > z))
+            def _():
+                right_copy(c, b).wait_send()
+
+            @pl.when(middle & (c < z))
+            def _():
+                left_copy(c, b).wait_send()
+        return carry
+
+    lax.fori_loop(0, blocks, drain, 0)
+
     def finish(n, carry):
         b = lax.rem(n + given, blocks)
         rows = pl.ds(pl.multiple_of(b * ROWS, ROWS), ROWS)
@@ -364,31 +402,20 @@
 
     lax.fori_loop(0, blocks, finish, 0)
 
-    chip_each(lambda copy: copy.wait_send())
-    for d in range(1, hops + 1):
-        @pl.when(i + 2 * d < n_loop)
-        def _():
-            id_chip(d).wait_send()
-
-        @pl.when((core == 1) & (i >= 2 * d))
-        def _():
-            for copy in down_copies(d):
-                copy.wait_send()
-
-        @pl.when((core == 0) & (i >= 2 * d - 2))
-        def _():
-            for copy in up_copies(d - 1):
-                copy.wait_send()
-
+    def drain_late(b, carry):
+        direct = (b >= given) | (chip != 2)
+
+        @pl.when((z == 0) & direct)
+        def _():
+            right_copy(1, b).wait_send()
+
+        @pl.when((z == n_tp - 1) & direct)
+        def _():
+            left_copy(n_tp - 2, b).wait_send()
+        return carry
+
+    lax.fori_loop(0, blocks, drain_late, 0)
     for n in range(given):
-        @pl.when((chip == 2) & (z == 0))
-        def _():
-            side_first(1, n).wait_send()
-
-        @pl.when((chip == 2) & (z == n_tp - 1))
-        def _():
-            side_first(n_tp - 2, n).wait_send()
-
         @pl.when((chip == 0) & (z == 0))
         def _():
             side_second(1, n).wait_send()
@@ -404,29 +431,6 @@
         @pl.when((chip == 0) & (z == n_tp - 2))
         def _():
             side_third(n_tp - 2, recv_l, l_sem, n).wait_send()
-
-    def drain(b, carry):
-        direct = (b >= given) | (chip != 2)
-
-        @pl.when((z == 0) & direct)
-        def _():
-            right_copy(1, b).wait_send()
-
-        @pl.when((z == n_tp - 1) & direct)
-        def _():
-            left_copy(n_tp - 2, b).wait_send()
-
-        for c in range(n_tp):
-            @pl.when(middle & (c > z))
-            def _():
-                right_copy(c, b).wait_send()
-
-            @pl.when(middle & (c < z))
-            def _():
-                left_copy(c, b).wait_send()
-        return carry
-
-    lax.fori_loop(0, blocks, drain, 0)
 
 
 def per_device(queries, key_values, prompt_ids, out_weight):

time: 47.1 us -> 47.1 us (level)
  no operation moved by 1% of the time
where the time goes in v8:
time: 47.1 us; the launch traced here: 46.2 us
  Pallas kernels  45.4 us (96%)
  local copies, waits for them, and re-layouts  0.8 us (2%)
    pallas_call x1, Pallas kernels, per_device(): pl.pallas_call(functools.partial(kernel, n_loop, n_tp, reach), out_shape=...  45.4 us

profile of v8, /device:TPU:21, one launch (start us, length us, event | category | flops | bytes accessed | tf_op | source)
XLA Modules:
  0.0 46.2 jit_solution(2455693168632853284)
XLA Ops:
  0.0 45.4 %shard_map.46 = bf16[256,1024]{1,0:T(8,128)(2,1)S(1)} custom-call(bf16[256,1024]{1,0:T(8,128)(2,1)} %q_hbm.1, bf16[256,256]{1,0:T(8,128)(2,1)} %kv_hbm.1, s32[1,256]{1,0:T(1,128)} %bitcast.1, bf16[1024,4096]{1,0:T(8,128)(2,1)} %w_hbm.1), custom_call_target="tpu_custom_call" | custom-call | flops 3500000000 | bytes 10000000 | tf_op jit(solution)/shard_map/pallas_call | solution.py:448
  45.4 0.8 %copy.6 = bf16[256,1024]{1,0:T(8,128)(2,1)} copy(bf16[256,1024]{1,0:T(8,128)(2,1)S(1)} %shard_map.46) | data formatting | bytes 1048576

commit v9 on v8

--- a/solution.py
+++ b/solution.py
@@ -297,18 +297,33 @@
 
     lax.fori_loop(0, blocks + 2, step, 0)
 
-    def send_late(near, copy, step):
-        for n in range(given):
-            @pl.when(chip == 0)
-            def _():
+    def send_some(near, copy, step):
+        if not given:
+            copy(near, 0).start()
+            return
+
+        @pl.when(chip == 0)
+        def _():
+            for n in range(given):
                 side_first(near, n).wait_recv()
                 side_second(step, n).start()
 
-            @pl.when(chip != 2)
-            def _():
-                copy(near, n).start()
-        for late in range(given, blocks):
-            copy(near, late).start()
+        @pl.when(chip == 2)
+        def _():
+            copy(near, given).start()
+
+        @pl.when(chip != 2)
+        def _():
+            copy(near, 0).start()
+
+    def send_rest(near, copy):
+        for late in range(1, blocks):
+            if 0 < late <= given:
+                @pl.when(chip != 2)
+                def _():
+                    copy(near, late).start()
+            else:
+                copy(near, late).start()
 
     @pl.when(z == 0)
     def _():
@@ -316,7 +331,8 @@
             for c in range(n_tp - 1, 1, -1):
                 right_copy(c, b).wait_send()
             if b == blocks - 2:
-                send_late(1, right_copy, 1)
+                send_some(1, right_copy, 1)
+        send_rest(1, right_copy)
 
     @pl.when(z == n_tp - 1)
     def _():
@@ -324,7 +340,8 @@
             for c in range(n_tp - 2):
                 left_copy(c, b).wait_send()
             if b == blocks - 2:
-                send_late(n_tp - 2, left_copy, -1)
+                send_some(n_tp - 2, left_copy, -1)
+        send_rest(n_tp - 2, left_copy)
 
     for n in range(given):
         @pl.when((chip == 0) & (z == 1))

time: 47.1 us -> 47.1 us (level)
  no operation moved by 1% of the time
where the time goes in v9:
time: 47.1 us; the launch traced here: 46.2 us
  Pallas kernels  45.4 us (96%)
  local copies, waits for them, and re-layouts  0.8 us (2%)
    pallas_call x1, Pallas kernels, per_device(): pl.pallas_call(functools.partial(kernel, n_loop, n_tp, reach), out_shape=...  45.4 us

profile of v9, /device:TPU:21, one launch (start us, length us, event | category | flops | bytes accessed | tf_op | source)
XLA Modules:
  0.0 46.2 jit_solution(585983431694419839)
XLA Ops:
  0.0 45.4 %shard_map.46 = bf16[256,1024]{1,0:T(8,128)(2,1)S(1)} custom-call(bf16[256,1024]{1,0:T(8,128)(2,1)} %q_hbm.1, bf16[256,256]{1,0:T(8,128)(2,1)} %kv_hbm.1, s32[1,256]{1,0:T(1,128)} %bitcast.1, bf16[1024,4096]{1,0:T(8,128)(2,1)} %w_hbm.1), custom_call_target="tpu_custom_call" | custom-call | flops 3500000000 | bytes 10000000 | tf_op jit(solution)/shard_map/pallas_call | solution.py:465
  45.4 0.8 %copy.6 = bf16[256,1024]{1,0:T(8,128)(2,1)} copy(bf16[256,1024]{1,0:T(8,128)(2,1)S(1)} %shard_map.46) | data formatting | bytes 1048576

commit v10 on v8

--- a/solution.py
+++ b/solution.py
@@ -11,7 +11,7 @@
 HD = 128
 BLOCKED = -1e30
 ROWS = 32
-STACK = 4
+STACK = 8
 MESH = pl.DeviceIdType.MESH
 
 

time: 47.1 us -> 47.3 us (level)
  no operation moved by 1% of the time
where the time goes in v10:
time: 47.3 us; the launch traced here: 46.5 us
  Pallas kernels  45.7 us (97%)
  local copies, waits for them, and re-layouts  0.8 us (2%)
    pallas_call x1, Pallas kernels, per_device(): pl.pallas_call(functools.partial(kernel, n_loop, n_tp, reach), out_shape=...  45.7 us

profile of v10, /device:TPU:21, one launch (start us, length us, event | category | flops | bytes accessed | tf_op | source)
XLA Modules:
  0.0 46.5 jit_solution(18088945634560914834)
XLA Ops:
  0.0 45.7 %shard_map.46 = bf16[256,1024]{1,0:T(8,128)(2,1)S(1)} custom-call(bf16[256,1024]{1,0:T(8,128)(2,1)} %q_hbm.1, bf16[256,256]{1,0:T(8,128)(2,1)} %kv_hbm.1, s32[1,256]{1,0:T(1,128)} %bitcast.1, bf16[1024,4096]{1,0:T(8,128)(2,1)} %w_hbm.1), custom_call_target="tpu_custom_call" | custom-call | flops 3500000000 | bytes 10000000 | tf_op jit(solution)/shard_map/pallas_call | solution.py:448
  45.7 0.8 %copy.6 = bf16[256,1024]{1,0:T(8,128)(2,1)} copy(bf16[256,1024]{1,0:T(8,128)(2,1)S(1)} %shard_map.46) | data formatting | bytes 1048576
